TPU v7x, 256 devices: a whole 4x4x8 slice. The times are simulated.
256 devices in a mesh: dp: 64 (over z, x, core), tensor: 4 (over y).
Axes of the slice: x: 4, y: 4, z: 8, core: 2. Of those that a mesh axis runs over, the one named last changes fastest.
Arguments:
- grads: bfloat16 [2, 64, 128, 12800], P(None, 'dp', None, 'tensor'), may hold values from -16 to 16, as said below
- errors: float32 [2, 64, 128, 12800], P(None, 'dp', None, 'tensor'), may hold values from -4 to 4
- q_prev: float32 [2, 32, 12800], P(None, None, 'tensor'), may hold values from -0.0546875 to 0.0546875
Outputs:
- rebuilt: bfloat16 [2, 128, 12800], P(None, None, 'tensor')
- new_errors: float32 [2, 64, 128, 12800], P(None, 'dp', None, 'tensor')
- new_q: float32 [2, 32, 12800], P(None, None, 'tensor')
Inputs may be any that keep to these rules, and one draw needn't show every extreme that they name: `grads`: each replica's gradient.
All inputs are finite; a program needn't handle non-finite values.
Results may differ from a plain program's by a relative error of at most 0.001.
Values sent between devices are 32-bit elements; how exact they have to be, the bound alone decides.
No kernel may reach another device: no remote copies, remote signals or barrier semaphores. Data moves between devices by JAX's collectives and lax.ppermute only.
A program may use at most 64 MiB of HBM per device.

v0:
```python
import jax
import jax.numpy as jnp
from jax import lax
from jax.sharding import PartitionSpec as P


def left_terms(corrected, q_one):
    return jnp.einsum("rf,kf->rk", corrected, q_one, precision=lax.Precision.HIGHEST)


def orthonormal(left):
    gram = jnp.dot(left.T, left, precision=lax.Precision.HIGHEST)
    chol = jnp.linalg.cholesky(gram)
    return jax.scipy.linalg.solve_triangular(chol, left.T, lower=True).T


def right_terms(corrected, ortho):
    return jnp.einsum("rf,rk->kf", corrected, ortho, precision=lax.Precision.HIGHEST)


def finish(corrected, ortho, summed, replicas):
    new_q = summed / replicas
    approx = jnp.dot(ortho, new_q, precision=lax.Precision.HIGHEST)
    return (approx.astype(jnp.bfloat16), (corrected - approx)[None], new_q)


def shards(grads, errors, q_prev):
    replicas = lax.axis_size("dp")
    first = grads[0, 0].astype(jnp.float32) + errors[0, 0]
    second = grads[1, 0].astype(jnp.float32) + errors[1, 0]
    results = []
    for corrected, q_one in ((first, q_prev[0]), (second, q_prev[1])):
        left = lax.psum(left_terms(corrected, q_one), ("dp", "tensor"))
        ortho = orthonormal(left)
        summed = lax.psum(right_terms(corrected, ortho), "dp")
        results.append(finish(corrected, ortho, summed, replicas))
    rebuilt = jnp.stack([results[0][0], results[1][0]])
    new_errors = jnp.stack([results[0][1], results[1][1]])
    new_q = jnp.stack([results[0][2], results[1][2]])
    return (rebuilt, new_errors, new_q)


def solution(mesh):
    in_specs = (
        P(None, "dp", None, "tensor"),
        P(None, "dp", None, "tensor"),
        P(None, None, "tensor"),
    )
    out_specs = (P(None, None, "tensor"), P(None, "dp", None, "tensor"), P(None, None, "tensor"))
    return jax.shard_map(shards, mesh=mesh, in_specs=in_specs, out_specs=out_specs, check_vma=False)
```

profile of v0, /device:TPU:1, one launch (start us, length us, event | category | flops | bytes accessed | tf_op | source)
XLA Modules:
  0.0 309.2 jit_solution(6999258846193281771)
XLA Ops:
  7.2 0.0 all-reduce.4.cloned.1.call-start
  7.2 0.0 copy-start.1
  7.2 0.0 copy-start.6
  7.2 3.6 %fusion.2 = f32[128,32]{0,1:T(8,128)S(1)} fusion(f32[2,32,3200]{2,1,0:T(8,128)} %param.8, f32[2,1,128,3200]{3,2,1,0:T(8,128)} %param.7, bf16[2,1,128,3200]{3,2,1,0:T(8,128)(2,1)} %param.6), kind=kOutput, calls=%fused_computation.5 | convolution fusion | flops 158105600 | bytes 2883584 | tf_op jit(solution)/shard_map/rf,kf->rk/dot_general | solution.py:8
  10.8 0.0 copy-done.1
  10.9 0.0 copy-start
  10.9 3.3 %fusion.7 = f32[128,32]{0,1:T(8,128)S(1)} fusion(f32[2,32,3200]{2,1,0:T(8,128)S(1)} %copy-done.6, f32[2,1,128,3200]{3,2,1,0:T(8,128)} %param.7, bf16[2,1,128,3200]{3,2,1,0:T(8,128)(2,1)S(1)} %copy-done.1), kind=kOutput, calls=%fused_computation.11 | convolution fusion | flops 158105600 | bytes 2883584 | tf_op jit(solution)/shard_map/rf,kf->rk/dot_general | solution.py:8
  14.2 81.6 %all-reduce = (f32[128,32]{0,1:T(8,128)S(1)}, f32[128,32]{0,1:T(8,128)S(1)}) all-reduce(f32[128,32]{0,1:T(8,128)S(1)} %fusion.2, f32[128,32]{0,1:T(8,128)S(1)} %fusion.7), channel_id=1, replica_groups=mesh['dp'=64,'tensor'=4] {'dp','tensor'}, use_global_device_ids=true, to_apply=%region_4.7 | all-reduce | flops 8192 | bytes 65536 | tf_op jit(solution)/shard_map/psum | solution.py:33
  95.8 0.1 fusion.35
  95.9 0.1 fusion.34
  96.1 0.1 copy.6
  96.2 2.9 cholesky.44
  99.1 0.6 compare_reduce_fusion.1
  99.8 0.7 fusion.20
  100.4 2.4 custom-call.6
  102.9 0.2 fusion.26
  103.1 0.1 copy.7
  103.2 2.9 cholesky.55
  106.1 0.6 compare_reduce_fusion
  106.8 0.7 fusion.21
  107.4 2.4 custom-call.7
  109.9 0.2 fusion.22
  110.1 3.1 fusion
  113.2 1.8 fusion.5
  115.0 0.0 all-reduce.4.cloned.1.call-update
  115.1 178.4 %all-reduce.4.cloned.1.call-done = (f32[32,3200]{1,0:T(8,128)}, f32[32,3200]{1,0:T(8,128)}) async-done(((f32[32,3200]{1,0:T(8,128)}, f32[32,3200]{1,0:T(8,128)}), (f32[32,3200]{1,0:T(8,128)}, f32[32,3200]{1,0:T(8,128)})) %all-reduce.4.cloned.1.call-update) | async-done | bytes 819216 | tf_op jit(solution)/shard_map/psum | solution.py:35
  293.5 2.6 fusion.14
  296.1 0.1 multiply_bitcast_fusion
  296.2 1.9 fusion.9
  298.1 0.9 pad_maximum_fusion.2
  299.1 1.9 pad_maximum_fusion
  301.0 1.3 pad_maximum_fusion.1
  (14 shorter events, 0.1 us)
Async XLA Ops:
  7.2 286.3 %all-reduce.4.cloned.1.call-start = ((), (), s32[]{:S(2)}) async-start(), calls=%async_computation | async-start | bytes 1638400 | tf_op jit(solution)/shard_map/psum | solution.py:35
  7.2 3.6 %copy-start.1 = (bf16[2,1,128,3200]{3,2,1,0:T(8,128)(2,1)S(1)}, bf16[2,1,128,3200]{3,2,1,0:T(8,128)(2,1)}, u32[]{:S(2)}) copy-start(bf16[2,1,128,3200]{3,2,1,0:T(8,128)(2,1)} %param.6) | copy-start | bytes 4915204
  7.2 3.6 %copy-start.6 = (f32[2,32,3200]{2,1,0:T(8,128)S(1)}, f32[2,32,3200]{2,1,0:T(8,128)}, u32[]{:S(2)}) copy-start(f32[2,32,3200]{2,1,0:T(8,128)} %param.8) | copy-start | bytes 2457604
  10.9 99.2 %copy-start = (f32[2,1,128,3200]{3,2,1,0:T(8,128)S(1)}, f32[2,1,128,3200]{3,2,1,0:T(8,128)}, u32[]{:S(2)}) copy-start(f32[2,1,128,3200]{3,2,1,0:T(8,128)} %param.7) | copy-start | bytes 9830404
  109.9 3.3 %copy-start.2 = (bf16[2,1,128,3200]{3,2,1,0:T(8,128)(2,1)S(1)}, bf16[2,1,128,3200]{3,2,1,0:T(8,128)(2,1)}, u32[]{:S(2)}) copy-start(bf16[2,1,128,3200]{3,2,1,0:T(8,128)(2,1)} %param.6) | copy-start | bytes 4915204
  293.5 2.6 copy-start.4
  293.5 2.7 copy-start.5
  293.5 2.7 copy-start.3
Sparse Core Ops, SparseCore 0:
  115.2 178.2 all-reduce.3
where the time goes:
time: 309 us
  waiting for transfers between devices  178 us (58%)
  blocking collectives  81.6 us (26%)
  other arithmetic  17.6 us (6%)
  matrix products  17.1 us (6%)
  between operations  14.2 us (5%)
    psum x1, waiting for transfers between devices, shards(): summed = lax.psum(right_terms(corrected, ortho), 'dp')  178 us
    psum x1, blocking collectives, shards(): left = lax.psum(left_terms(corrected, q_one), ('dp', 'tensor'))  81.6 us
    another operation x6, other arithmetic, orthonormal(): chol = jnp.linalg.cholesky(gram)  7.2 us
    dot_general x2, matrix products, left_terms(): jnp.einsum('rf,kf->rk', corrected, q_one, precision=lax.Precision.HIGHEST)  6.92 us
  transfers between devices with their start and end apart: 1, of which 1 were waited for; matrix products, arithmetic and copies ran while one was open for 0% of the time, Pallas kernels for 0%

commit v1 on v0

v1 whole, which is shorter than its diff:
```python
import jax
import jax.numpy as jnp
from jax import lax
from jax.experimental import pallas as pl
from jax.experimental.pallas import tpu as pltpu
from jax.sharding import Mesh
from jax.sharding import PartitionSpec as P

F32 = jnp.float32
BF16 = jnp.bfloat16
SIZES = {"z": 8, "x": 4, "core": 2, "tensor": 4}
RANK = 32
ROWS = 128
COLS = 3200
TILE = 640
VMEM_BYTES = 24 * 1024 * 1024


def params():
    return pltpu.CompilerParams(vmem_limit_bytes=VMEM_BYTES)


def split(value):
    high = value.astype(BF16)
    return high, (value - high.astype(F32)).astype(BF16)


def matmul(a, b, dims):
    return lax.dot_general(a, b, (dims, ((), ())), preferred_element_type=F32)


def correct_kernel(core_ref, g_own, g_oth, e_own, e_oth, q_own, q_oth, c_own, c_oth, left_own, left_oth):
    step = pl.program_id(0)
    for g, e, q, c_out, left in (
        (g_oth, e_oth, q_oth, c_oth, left_oth),
        (g_own, e_own, q_own, c_own, left_own),
    ):
        c = g[0, 0].astype(F32) + e[0, 0]
        c_out[...] = c
        c_hi, c_lo = split(c)
        q_hi, q_lo = split(q[0])
        both = matmul(jnp.concatenate([q_hi, q_lo], axis=0), c_hi, ((1,), (1,)))
        part = both[:RANK] + both[RANK:] + matmul(q_hi, c_lo, ((1,), (1,)))
        before = jnp.where(step == 0, jnp.zeros_like(part), left[...])
        left[...] = before + part


def correct(core, grads, errors, q_prev):
    own = lambda j, s: (s[0], 0, 0, j)
    oth = lambda j, s: (1 - s[0], 0, 0, j)
    own3 = lambda j, s: (s[0], 0, j)
    oth3 = lambda j, s: (1 - s[0], 0, j)
    block = (1, 1, ROWS, TILE)
    grid_spec = pltpu.PrefetchScalarGridSpec(
        num_scalar_prefetch=1,
        grid=(COLS // TILE,),
        in_specs=[
            pl.BlockSpec(block, own),
            pl.BlockSpec(block, oth),
            pl.BlockSpec(block, own),
            pl.BlockSpec(block, oth),
            pl.BlockSpec((1, RANK, TILE), own3),
            pl.BlockSpec((1, RANK, TILE), oth3),
        ],
        out_specs=[
            pl.BlockSpec((ROWS, TILE), lambda j, s: (0, j)),
            pl.BlockSpec((ROWS, TILE), lambda j, s: (0, j)),
            pl.BlockSpec((RANK, ROWS), lambda j, s: (0, 0)),
            pl.BlockSpec((RANK, ROWS), lambda j, s: (0, 0)),
        ],
    )
    return pl.pallas_call(
        correct_kernel,
        grid_spec=grid_spec,
        out_shape=[
            jax.ShapeDtypeStruct((ROWS, COLS), F32),
            jax.ShapeDtypeStruct((ROWS, COLS), F32),
            jax.ShapeDtypeStruct((RANK, ROWS), F32),
            jax.ShapeDtypeStruct((RANK, ROWS), F32),
        ],
        compiler_params=params(),
        name="correct",
    )(core, grads, grads, errors, errors, q_prev, q_prev)


def right_kernel(parts, c_own, c_got, raw, left):
    total = jnp.sum(parts[...], axis=0)
    left[...] = total
    l_hi, l_lo = split(total)
    s_hi, s_lo = split(c_own[...] + c_got[...])
    both = matmul(jnp.concatenate([l_hi, l_lo], axis=0), s_hi, ((1,), (0,)))
    value = both[:RANK] + both[RANK:] + matmul(l_hi, s_lo, ((1,), (0,)))
    for k in range(RANK):
        raw[k] = value[k : k + 1]


def right(parts, c_own, c_got):
    return pl.pallas_call(
        right_kernel,
        grid=(COLS // TILE,),
        in_specs=[
            pl.BlockSpec((SIZES["z"], RANK, ROWS), lambda j: (0, 0, 0)),
            pl.BlockSpec((ROWS, TILE), lambda j: (0, j)),
            pl.BlockSpec((ROWS, TILE), lambda j: (0, j)),
        ],
        out_specs=[
            pl.BlockSpec((RANK, 1, TILE), lambda j: (0, 0, j)),
            pl.BlockSpec((RANK, ROWS), lambda j: (0, 0)),
        ],
        out_shape=[
            jax.ShapeDtypeStruct((RANK, 1, COLS), F32),
            jax.ShapeDtypeStruct((RANK, ROWS), F32),
        ],
        compiler_params=params(),
        name="right_terms",
    )(parts, c_own, c_got)


def factor_kernel(left_ref, out):
    left = left_ref[...]
    gram = lax.dot_general(
        left, left, (((1,), (1,)), ((), ())), precision=lax.Precision.HIGHEST, preferred_element_type=F32
    )
    row = lax.broadcasted_iota(jnp.int32, (RANK, RANK), 0)
    col = lax.broadcasted_iota(jnp.int32, (RANK, RANK), 1)
    unit = (row == col).astype(F32)
    work = jnp.concatenate([gram, unit], axis=1)
    below = lax.broadcasted_iota(jnp.int32, (RANK, 2 * RANK), 0)
    for j in range(RANK):
        pivot_row = work[j : j + 1, :]
        pivot = work[j : j + 1, j : j + 1]
        scale = lax.rsqrt(pivot)
        scaled = pivot_row * scale
        column = work[:, j : j + 1] * scale
        work = jnp.where(below > j, work - column * scaled, jnp.where(below == j, scaled, work))
    inverse = work[:, RANK:]
    ortho = lax.dot_general(
        inverse, left, (((1,), (0,)), ((), ())), precision=lax.Precision.HIGHEST, preferred_element_type=F32
    )
    out[0] = ortho
    out[1] = jnp.concatenate([inverse, jnp.zeros((RANK, ROWS - RANK), F32)], axis=1)


def factor(left):
    return pl.pallas_call(
        factor_kernel,
        out_shape=jax.ShapeDtypeStruct((2, RANK, ROWS), F32),
        compiler_params=params(),
        cost_estimate=pl.CostEstimate(flops=10_000_000, bytes_accessed=10_000_000, transcendentals=0),
        name="factor",
    )(left)


def finish_kernel(which_ref, raw, factors, c, *refs):
    rebuilt, new_errors, new_q = refs[-3:]
    rows = jnp.concatenate([raw[k] for k in range(RANK)], axis=0)
    r_hi, r_lo = split(rows)
    i_hi, i_lo = split(factors[1][:, :RANK])
    q = matmul(
        jnp.concatenate([i_hi, i_hi, i_lo], axis=1), jnp.concatenate([r_hi, r_lo, r_hi], axis=0), ((1,), (0,))
    ) * (1.0 / (SIZES["z"] * SIZES["x"] * SIZES["core"]))
    new_q[0] = q
    q_hi, q_lo = split(q)
    o_hi, o_lo = split(factors[0])
    approx = matmul(
        jnp.concatenate([o_hi, o_hi, o_lo], axis=0), jnp.concatenate([q_hi, q_lo, q_hi], axis=0), ((0,), (0,))
    )
    rebuilt[0] = approx.astype(BF16)
    new_errors[0, 0] = c[...] - approx


def finish(which, raw, factors, c, held=()):
    grid_spec = pltpu.PrefetchScalarGridSpec(
        num_scalar_prefetch=1,
        grid=(COLS // TILE,),
        in_specs=[
            pl.BlockSpec((RANK, 1, TILE), lambda j, s: (0, 0, j)),
            pl.BlockSpec((2, RANK, ROWS), lambda j, s: (0, 0, 0)),
            pl.BlockSpec((ROWS, TILE), lambda j, s: (0, j)),
        ]
        + [pl.BlockSpec(memory_space=pl.ANY)] * len(held),
        out_specs=[
            pl.BlockSpec((1, ROWS, TILE), lambda j, s: (s[0], 0, j)),
            pl.BlockSpec((1, 1, ROWS, TILE), lambda j, s: (s[0], 0, 0, j)),
            pl.BlockSpec((1, RANK, TILE), lambda j, s: (s[0], 0, j)),
        ],
    )
    return pl.pallas_call(
        finish_kernel,
        grid_spec=grid_spec,
        out_shape=[
            jax.ShapeDtypeStruct((2, ROWS, COLS), BF16),
            jax.ShapeDtypeStruct((2, 1, ROWS, COLS), F32),
            jax.ShapeDtypeStruct((2, RANK, COLS), F32),
        ],
        input_output_aliases={4 + i: i for i in range(len(held))},
        compiler_params=params(),
        cost_estimate=pl.CostEstimate(flops=50_000_000, bytes_accessed=6_000_000, transcendentals=0),
        name="finish_second" if held else "finish_first",
    )(which, raw, factors, c, *held)


def swap(value):
    return lax.ppermute(value, "core", [(0, 1), (1, 0)])


def copies(value, axes):
    count = 1
    for axis in axes:
        count *= SIZES[axis]
    return lax.all_to_all(jnp.broadcast_to(value[None], (count,) + value.shape), axes, 0, 0, tiled=True)


def shards(grads, errors, q_prev):
    core = lax.axis_index("core").astype(jnp.int32)
    c_own, c_oth, left_own, left_oth = correct(core[None], grads, errors, q_prev)
    left = left_own + swap(left_oth)
    c_got = swap(c_oth)
    left = jnp.sum(copies(left, ("x", "tensor")), axis=0)
    parts = copies(left, ("z",))
    raw, left = right(parts, c_own, c_got)
    factors = factor(left)
    factors_got = swap(factors)
    mine = jnp.sum(lax.all_to_all(raw, ("z", "x"), 0, 0, tiled=True), axis=0)
    raw = copies(mine, ("z", "x"))
    raw_got = swap(raw)
    outs = finish(core[None], raw, factors, c_own)
    return tuple(finish(1 - core[None], raw_got, factors_got, c_oth, outs))


def solution(mesh):
    fine = Mesh(mesh.devices.reshape(tuple(SIZES.values())), tuple(SIZES))
    dp = ("z", "x", "core")
    in_specs = (
        P(None, dp, None, "tensor"),
        P(None, dp, None, "tensor"),
        P(None, None, "tensor"),
    )
    out_specs = (P(None, None, "tensor"), P(None, dp, None, "tensor"), P(None, None, "tensor"))
    return jax.shard_map(shards, mesh=fine, in_specs=in_specs, out_specs=out_specs, check_vma=False)
```

time: 309 us -> 95.6 us (0.31)
  waiting for transfers between devices: 178 us -> 3.02 us
  blocking collectives: 81.6 us -> 60.4 us
  other arithmetic: 17.6 us -> 0.26 us
  Pallas kernels: 0 us -> 17.3 us
  matrix products: 17.1 us -> 0 us
  between operations: 14.2 us -> 0.69 us
  starting transfers between devices: 0.04 us -> 8.74 us
  local copies, waits for them, and re-layouts: 0.18 us -> 4.74 us
    psum x1 -> x0, waiting for transfers between devices: 178 us -> none  [shards(): summed = lax.psum(right_terms(corrected, ortho), 'dp')]
    psum x1 -> x0, blocking collectives: 81.6 us -> none  [shards(): left = lax.psum(left_terms(corrected, q_one), ('dp', 'tensor'))]
    all_to_all x0 -> x4, blocking collectives: none -> 60.4 us  [the longest x3 45.4 us: copies(): lax.all_to_all(jnp.broadcast_to(value[None], (count,) + value.shape), axe...]
    another operation x14 -> x0, other arithmetic: 17.6 us -> none  [the longest x6 7.2 us: orthonormal(): chol = jnp.linalg.cholesky(gram)]
    pallas_call x0 -> x5, Pallas kernels: none -> 17.3 us  [the longest x2 9.14 us: finish(): pl.pallas_call(finish_kernel, grid_spec=grid_spec, out_shape=[jax.ShapeDt...]
    dot_general x8 -> x0, matrix products: 16.7 us -> none  [the longest x2 6.92 us: left_terms(): jnp.einsum('rf,kf->rk', corrected, q_one, precision=lax.Precision.HIGHEST)]
    ppermute x0 -> x4, starting transfers between devices: none -> 8.74 us  [swap(): return lax.ppermute(value, 'core', [(0, 1), (1, 0)])]
    unnamed x14 -> x6, local copies, waits for them, and re-layouts: 0.04 us -> 4.49 us
  transfers between devices with their start and end apart: 1 -> 4, of which waited for: 1 -> 1; matrix products, arithmetic and copies ran while one was open for 0% -> 0% of each run, Pallas kernels for 0% -> 7%
where the time goes in v1:
time: 95.6 us; the launch traced here: 95.2 us
  blocking collectives  60.4 us (63%)
  Pallas kernels  17.3 us (18%)
  starting transfers between devices  8.74 us (9%)
  local copies, waits for them, and re-layouts  4.74 us (5%)
  waiting for transfers between devices  3.02 us (3%)
    all_to_all x3, blocking collectives, copies(): lax.all_to_all(jnp.broadcast_to(value[None], (count,) + value.shape), axe...  45.4 us
    all_to_all x1, blocking collectives, shards(): mine = jnp.sum(lax.all_to_all(raw, ('z', 'x'), 0, 0, tiled=True), axis=0)  15.1 us
    pallas_call x2, Pallas kernels, finish(): pl.pallas_call(finish_kernel, grid_spec=grid_spec, out_shape=[jax.ShapeDt...  9.14 us
    ppermute x4, starting transfers between devices, swap(): return lax.ppermute(value, 'core', [(0, 1), (1, 0)])  8.74 us
    unnamed x6, local copies, waits for them, and re-layouts  4.49 us
    pallas_call x1, Pallas kernels, correct(): pl.pallas_call(correct_kernel, grid_spec=grid_spec, out_shape=[jax.ShapeD...  3.77 us
    ppermute x4, waiting for transfers between devices, swap(): return lax.ppermute(value, 'core', [(0, 1), (1, 0)])  3.02 us
    pallas_call x1, Pallas kernels, factor(): pl.pallas_call(factor_kernel, out_shape=jax.ShapeDtypeStruct((2, RANK, RO...  2.98 us
  transfers between devices with their start and end apart: 4, of which 1 were waited for; matrix products, arithmetic and copies ran while one was open for 0% of the time, Pallas kernels for 7%

profile of v1, /device:TPU:1, one launch (start us, length us, event | category | flops | bytes accessed | tf_op | source)
XLA Modules:
  0.0 95.2 jit_solution(6475160567591108440)
XLA Ops:
  0.6 0.0 copy-start
  0.6 1.9 %copy-done = f32[2,1,128,3200]{3,2,1,0:T(8,128)S(1)} copy-done((f32[2,1,128,3200]{3,2,1,0:T(8,128)S(1)}, f32[2,1,128,3200]{3,2,1,0:T(8,128)}, u32[]{:S(2)}) %copy-start) | copy-done | bytes 3276824
  2.6 0.0 copy-start.1
  2.6 1.4 %copy-done.1 = bf16[2,1,128,3200]{3,2,1,0:T(8,128)(2,1)S(1)} copy-done((bf16[2,1,128,3200]{3,2,1,0:T(8,128)(2,1)S(1)}, bf16[2,1,128,3200]{3,2,1,0:T(8,128)(2,1)}, u32[]{:S(2)}) %copy-start.1) | copy-done | bytes 1638424
  4.0 0.0 copy-start.2
  4.0 1.1 %copy-done.2 = f32[2,32,3200]{2,1,0:T(8,128)S(1)} copy-done((f32[2,32,3200]{2,1,0:T(8,128)S(1)}, f32[2,32,3200]{2,1,0:T(8,128)}, u32[]{:S(2)}) %copy-start.2) | copy-done | bytes 819224
  5.1 3.8 %correct.1 = (f32[128,3200]{1,0:T(8,128)S(1)}, f32[128,3200]{1,0:T(8,128)}, f32[32,128]{1,0:T(8,128)S(1)}, f32[32,128]{1,0:T(8,128)S(1)}) custom-call(s32[1]{0:T(128)} %bitcast.core_ref.which_ref, bf16[2,1,128,3200]{3,2,1,0:T(8,128)(2,1)S(1)} %copy-done.1, bf16[2,1,128,3200]{3,2,1,0:T(8,128)(2,1)S(1)} %copy-done.1, f32[2,1,128,3200]{3,2,1,0:T(8,128)S(1)} %copy-done, ...), custom_call_target="tpu_custom_call" | custom-call | tf_op jit(solution)/shard_map/correct/pallas_call | solution.py:72
  8.9 3.2 %collective-permute-start.1 = (f32[128,3200]{1,0:T(8,128)}, f32[128,3200]{1,0:T(8,128)S(1)}, u32[]{:S(2)}, u32[]{:S(2)}) collective-permute-start(f32[128,3200]{1,0:T(8,128)} %get-tuple-element.15.c), channel_id=1, source_target_pairs={{0,4},{4,0},{1,5},{5,1},{2,6},{6,2},{3,7},{7,3},{8,12},{12,8},{9,1... | collective-permute-start | bytes 4915208 | tf_op jit(solution)/shard_map/ppermute | solution.py:204
  12.1 0.0 collective-permute-start
  12.1 3.0 %collective-permute-done = f32[32,128]{1,0:T(8,128)S(1)} collective-permute-done((f32[32,128]{1,0:T(8,128)S(1)}, f32[32,128]{1,0:T(8,128)S(1)}, u32[]{:S(2)}, u32[]{:S(2)}) %collective-permute-start) | collective-permute-done | bytes 16416 | tf_op jit(solution)/shard_map/ppermute | solution.py:204
  15.2 12.6 %all_to_all.20 = f32[16,32,128]{2,1,0:T(8,128)S(1)} all-to-all(f32[16,32,128]{2,1,0:T(8,128)S(1)} %broadcast_in_dim.9), channel_id=1, replica_groups=mesh['z'=8,'x'=4,'core'=2,'tensor'=4] {'x','tensor'}, dimensions={0} | all-to-all | bytes 524288 | tf_op jit(solution)/shard_map/all_to_all | solution.py:211
  27.8 16.0 %all_to_all.21.parts = f32[8,32,128]{2,1,0:T(8,128)S(1)} all-to-all(f32[8,32,128]{2,1,0:T(8,128)S(1)} %broadcast_in_dim.10), channel_id=1, replica_groups=mesh['z'=8,'x'=4,'core'=2,'tensor'=4] {'z'}, dimensions={0} | all-to-all | bytes 262144 | tf_op jit(solution)/shard_map/all_to_all | solution.py:211
  43.8 0.0 collective-permute-done.1.c_got
  43.9 1.4 %right_terms.1 = (f32[32,1,3200]{2,1,0:T(1,128)S(1)}, f32[32,128]{1,0:T(8,128)S(1)}) custom-call(f32[8,32,128]{2,1,0:T(8,128)S(1)} %all_to_all.21.parts, f32[128,3200]{1,0:T(8,128)S(1)} %get-tuple-element.14.c_own.c, f32[128,3200]{1,0:T(8,128)S(1)} %collective-permute-done.1.c_got), custom_call_target="tpu_custom_call" | custom-call | tf_op jit(solution)/shard_map/right_terms/pallas_call | solution.py:98
  45.3 15.1 %all_to_all.22 = f32[32,1,3200]{2,1,0:T(1,128)S(1)} all-to-all(f32[32,1,3200]{2,1,0:T(1,128)S(1)} %get-tuple-element.16), channel_id=1, replica_groups=mesh['z'=8,'x'=4,'core'=2,'tensor'=4] {'z','x'}, dimensions={0} | all-to-all | bytes 819200 | tf_op jit(solution)/shard_map/all_to_all | solution.py:224
  60.4 0.2 reduce_sum.19
  60.6 0.2 broadcast_in_dim.11
  60.8 16.7 %all_to_all.23.raw = f32[32,1,3200]{2,1,0:T(1,128)S(1)} all-to-all(f32[32,1,3200]{2,1,0:T(1,128)S(1)} %broadcast_in_dim.11), channel_id=1, replica_groups=mesh['z'=8,'x'=4,'core'=2,'tensor'=4] {'z','x'}, dimensions={0} | all-to-all | bytes 819200 | tf_op jit(solution)/shard_map/all_to_all | solution.py:211
  77.6 5.5 %collective-permute-start.2 = (f32[32,1,3200]{2,1,0:T(1,128)S(1)}, f32[32,1,3200]{2,1,0:T(1,128)S(1)}, u32[]{:S(2)}, u32[]{:S(2)}) collective-permute-start(f32[32,1,3200]{2,1,0:T(1,128)S(1)} %all_to_all.23.raw), channel_id=1, source_target_pairs={{0,4},{4,0},{1,5},{5,1},{2,6},{6,2},{3,7},{7,3},{8,12},{12,8},{9,1... | collective-permute-start | bytes 1228808 | tf_op jit(solution)/shard_map/ppermute | solution.py:204
  83.1 3.0 %factor.1.factors = f32[2,32,128]{2,1,0:T(8,128)S(1)} custom-call(f32[32,128]{1,0:T(8,128)S(1)} %get-tuple-element.17.left_ref), custom_call_target="tpu_custom_call" | custom-call | flops 10000000 | bytes 10000000 | tf_op jit(solution)/shard_map/factor/pallas_call | solution.py:145
  86.0 0.0 collective-permute-start.3
  86.1 3.7 %finish_first.1 = (bf16[2,128,3200]{2,1,0:T(8,128)(2,1)}, f32[2,1,128,3200]{3,2,1,0:T(8,128)}, f32[2,32,3200]{2,1,0:T(8,128)}) custom-call(s32[1]{0:T(128)} %bitcast.core_ref.which_ref, f32[32,1,3200]{2,1,0:T(1,128)S(1)} %all_to_all.23.raw, f32[2,32,128]{2,1,0:T(8,128)S(1)} %factor.1.factors, f32[128,3200]{1,0:T(8,128)S(1)} %get-tuple-element.14.c_own.c), custom_call_target="tpu_custom_call" | custom-call | flops 50000000 | bytes 6000000 | tf_op jit(solution)/shard_map/finish_first/pallas_call | solution.py:188
  89.8 0.0 collective-permute-done.3.factors
  89.8 0.0 collective-permute-done.2.raw
  89.8 5.4 %finish_second.1 = (bf16[2,128,3200]{2,1,0:T(8,128)(2,1)}, f32[2,1,128,3200]{3,2,1,0:T(8,128)}, f32[2,32,3200]{2,1,0:T(8,128)}) custom-call(s32[1]{0:T(128)S(6)} %sub.3.which_ref, f32[32,1,3200]{2,1,0:T(1,128)S(1)} %collective-permute-done.2.raw, ...), custom_call_target="tpu_custom_call", output_to_operand_aliasing={{0}: (4, {}), {1}: (5, {}), {2}: (6, {})} | custom-call | flops 50000000 | bytes 6000000 | tf_op jit(solution)/shard_map/finish_second/pallas_call | solution.py:188
  (4 shorter events, 0.1 us)
Async XLA Ops:
  0.6 1.9 %copy-start = (f32[2,1,128,3200]{3,2,1,0:T(8,128)S(1)}, f32[2,1,128,3200]{3,2,1,0:T(8,128)}, u32[]{:S(2)}) copy-start(f32[2,1,128,3200]{3,2,1,0:T(8,128)} %e_oth.1) | copy-start | bytes 9830404
  2.6 1.4 %copy-start.1 = (bf16[2,1,128,3200]{3,2,1,0:T(8,128)(2,1)S(1)}, bf16[2,1,128,3200]{3,2,1,0:T(8,128)(2,1)}, u32[]{:S(2)}) copy-start(bf16[2,1,128,3200]{3,2,1,0:T(8,128)(2,1)} %g_oth.1) | copy-start | bytes 4915204
  4.0 1.1 %copy-start.2 = (f32[2,32,3200]{2,1,0:T(8,128)S(1)}, f32[2,32,3200]{2,1,0:T(8,128)}, u32[]{:S(2)}) copy-start(f32[2,32,3200]{2,1,0:T(8,128)} %q_oth.1) | copy-start | bytes 2457604
  8.9 34.9 %collective-permute-start.1 = (f32[128,3200]{1,0:T(8,128)}, f32[128,3200]{1,0:T(8,128)S(1)}, u32[]{:S(2)}, u32[]{:S(2)}) collective-permute-start(f32[128,3200]{1,0:T(8,128)} %get-tuple-element.15.c), channel_id=1, source_target_pairs={{0,4},{4,0},{1,5},{5,1},{2,6},{6,2},{3,7},{7,3},{8,12},{12,8},{9,1... | collective-permute-start | bytes 4915208 | tf_op jit(solution)/shard_map/ppermute | solution.py:204
  12.1 3.0 %collective-permute-start = (f32[32,128]{1,0:T(8,128)S(1)}, f32[32,128]{1,0:T(8,128)S(1)}, u32[]{:S(2)}, u32[]{:S(2)}) collective-permute-start(f32[32,128]{1,0:T(8,128)S(1)} %get-tuple-element.13), channel_id=1, source_target_pairs={{0,4},{4,0},{1,5},{5,1},{2,6},{6,2},{3,7},{7,3},{8,12},{12,8},{9,1... | collective-permute-start | bytes 49160 | tf_op jit(solution)/shard_map/ppermute | solution.py:204
  77.6 12.2 %collective-permute-start.2 = (f32[32,1,3200]{2,1,0:T(1,128)S(1)}, f32[32,1,3200]{2,1,0:T(1,128)S(1)}, u32[]{:S(2)}, u32[]{:S(2)}) collective-permute-start(f32[32,1,3200]{2,1,0:T(1,128)S(1)} %all_to_all.23.raw), channel_id=1, source_target_pairs={{0,4},{4,0},{1,5},{5,1},{2,6},{6,2},{3,7},{7,3},{8,12},{12,8},{9,1... | collective-permute-start | bytes 1228808 | tf_op jit(solution)/shard_map/ppermute | solution.py:204
  86.0 3.8 %collective-permute-start.3 = (f32[2,32,128]{2,1,0:T(8,128)S(1)}, f32[2,32,128]{2,1,0:T(8,128)S(1)}, u32[]{:S(2)}, u32[]{:S(2)}) collective-permute-start(f32[2,32,128]{2,1,0:T(8,128)S(1)} %factor.1.factors), channel_id=1, source_target_pairs={{0,4},{4,0},{1,5},{5,1},{2,6},{6,2},{3,7},{7,3},{8,12},{12,8},{9,1... | collective-permute-start | bytes 98312 | tf_op jit(solution)/shard_map/ppermute | solution.py:204

commit v2 on v1

v2 whole, which is shorter than its diff:
```python
import jax
import jax.numpy as jnp
from jax import lax
from jax.experimental import pallas as pl
from jax.experimental.pallas import tpu as pltpu
from jax.sharding import Mesh
from jax.sharding import PartitionSpec as P

F32 = jnp.float32
BF16 = jnp.bfloat16
SIZES = {"z": 8, "x": 4, "core": 2, "tensor": 4}
RANK = 32
ROWS = 128
COLS = 3200
TILE = 640
CHUNKS = COLS // TILE
VMEM_BYTES = 24 * 1024 * 1024


def params():
    return pltpu.CompilerParams(vmem_limit_bytes=VMEM_BYTES)


def split(value):
    high = value.astype(BF16)
    return high, (value - high.astype(F32)).astype(BF16)


def matmul(a, b, dims):
    return lax.dot_general(a, b, (dims, ((), ())), preferred_element_type=F32)


def correct_kernel(core_ref, grads, errors, q_prev, c_own, c_oth, left_own, left_oth, g_buf, q_buf, sems):
    own = core_ref[0]
    copies_in = []
    for slot, (m, c_out) in enumerate(((1 - own, c_oth), (own, c_own))):
        copies_in.append([pltpu.make_async_copy(q_prev.at[m], q_buf.at[slot], sems.at[slot, 2 * CHUNKS])])
        for j in range(CHUNKS):
            cols = pl.ds(j * TILE, TILE)
            copies_in[slot].append(
                (
                    pltpu.make_async_copy(grads.at[m, 0, :, cols], g_buf.at[slot, j], sems.at[slot, j]),
                    pltpu.make_async_copy(errors.at[m, 0, :, cols], c_out.at[:, cols], sems.at[slot, CHUNKS + j]),
                )
            )
    for slot in range(2):
        copies_in[slot][0].start()
        for g_copy, e_copy in copies_in[slot][1:]:
            g_copy.start()
            e_copy.start()
    for slot, (c_out, left) in enumerate(((c_oth, left_oth), (c_own, left_own))):
        copies_in[slot][0].wait()
        total = jnp.zeros((RANK, ROWS), F32)
        for j in range(CHUNKS):
            cols = pl.ds(j * TILE, TILE)
            for copy in copies_in[slot][1 + j]:
                copy.wait()
            c = g_buf[slot, j].astype(F32) + c_out[:, cols]
            c_out[:, cols] = c
            c_hi, c_lo = split(c)
            q_hi, q_lo = split(q_buf[slot, :, cols])
            both = matmul(jnp.concatenate([q_hi, q_lo], axis=0), c_hi, ((1,), (1,)))
            total += both[:RANK] + both[RANK:] + matmul(q_hi, c_lo, ((1,), (1,)))
        left[...] = total


def in_vmem(count):
    return [pl.BlockSpec(memory_space=pltpu.VMEM)] * count


def anywhere(count):
    return [pl.BlockSpec(memory_space=pl.ANY)] * count


SCALAR = pl.BlockSpec(memory_space=pltpu.SMEM)


def correct(core, grads, errors, q_prev):
    return pl.pallas_call(
        correct_kernel,
        in_specs=[SCALAR] + [pl.BlockSpec(memory_space=pltpu.HBM)] * 3,
        out_specs=in_vmem(4),
        out_shape=[
            jax.ShapeDtypeStruct((ROWS, COLS), F32),
            jax.ShapeDtypeStruct((ROWS, COLS), F32),
            jax.ShapeDtypeStruct((RANK, ROWS), F32),
            jax.ShapeDtypeStruct((RANK, ROWS), F32),
        ],
        scratch_shapes=[
            pltpu.VMEM((2, CHUNKS, ROWS, TILE), BF16),
            pltpu.VMEM((2, RANK, COLS), F32),
            pltpu.SemaphoreType.DMA((2, 2 * CHUNKS + 1)),
        ],
        compiler_params=params(),
        cost_estimate=pl.CostEstimate(flops=300_000_000, bytes_accessed=9_000_000, transcendentals=0),
        name="correct",
    )(core, *[pltpu.with_memory_space_constraint(x, pltpu.HBM) for x in (grads, errors, q_prev)])


def right_kernel(parts, c_own, c_got, raw, left):
    total = jnp.sum(parts[...], axis=0)
    left[...] = total
    l_hi, l_lo = split(total)
    l_both = jnp.concatenate([l_hi, l_lo], axis=0)
    for j in range(CHUNKS):
        cols = pl.ds(j * TILE, TILE)
        s_hi, s_lo = split(c_own[:, cols] + c_got[:, cols])
        both = matmul(l_both, s_hi, ((1,), (0,)))
        value = both[:RANK] + both[RANK:] + matmul(l_hi, s_lo, ((1,), (0,)))
        for k in range(RANK):
            raw[k, :, cols] = value[k : k + 1]


def right(parts, c_own, c_got):
    return pl.pallas_call(
        right_kernel,
        in_specs=in_vmem(3),
        out_specs=in_vmem(2),
        out_shape=[
            jax.ShapeDtypeStruct((RANK, 1, COLS), F32),
            jax.ShapeDtypeStruct((RANK, ROWS), F32),
        ],
        compiler_params=params(),
        cost_estimate=pl.CostEstimate(flops=100_000_000, bytes_accessed=4_000_000, transcendentals=0),
        name="right_terms",
    )(parts, c_own, c_got)


def factor_kernel(left_ref, out):
    left = left_ref[...]
    gram = lax.dot_general(
        left, left, (((1,), (1,)), ((), ())), precision=lax.Precision.HIGHEST, preferred_element_type=F32
    )
    row = lax.broadcasted_iota(jnp.int32, (RANK, RANK), 0)
    col = lax.broadcasted_iota(jnp.int32, (RANK, RANK), 1)
    unit = (row == col).astype(F32)
    work = jnp.concatenate([gram, unit], axis=1)
    below = lax.broadcasted_iota(jnp.int32, (RANK, 2 * RANK), 0)
    for j in range(RANK):
        pivot_row = work[j : j + 1, :]
        pivot = work[j : j + 1, j : j + 1]
        scale = lax.rsqrt(pivot)
        scaled = pivot_row * scale
        column = work[:, j : j + 1] * scale
        work = jnp.where(below > j, work - column * scaled, jnp.where(below == j, scaled, work))
    inverse = work[:, RANK:]
    ortho = lax.dot_general(
        inverse, left, (((1,), (0,)), ((), ())), precision=lax.Precision.HIGHEST, preferred_element_type=F32
    )
    out[0] = ortho
    out[1] = jnp.concatenate([inverse, jnp.zeros((RANK, ROWS - RANK), F32)], axis=1)


def factor(left):
    return pl.pallas_call(
        factor_kernel,
        in_specs=in_vmem(1),
        out_specs=in_vmem(1)[0],
        out_shape=jax.ShapeDtypeStruct((2, RANK, ROWS), F32),
        compiler_params=params(),
        cost_estimate=pl.CostEstimate(flops=10_000_000, bytes_accessed=10_000_000, transcendentals=0),
        name="factor",
    )(left)


def finish_kernel(which_ref, raw, factors, c, *refs):
    rebuilt, new_errors, new_q, r_buf, e_buf, q_buf, sems = refs[-7:]
    m = which_ref[0]
    i_hi, i_lo = split(factors[1][:, :RANK])
    i_all = jnp.concatenate([i_hi, i_hi, i_lo], axis=1)
    o_hi, o_lo = split(factors[0])
    o_all = jnp.concatenate([o_hi, o_hi, o_lo], axis=0)
    out = []
    for j in range(CHUNKS):
        cols = pl.ds(j * TILE, TILE)
        rows = jnp.concatenate([raw[k, :, cols] for k in range(RANK)], axis=0)
        r_hi, r_lo = split(rows)
        q = matmul(i_all, jnp.concatenate([r_hi, r_lo, r_hi], axis=0), ((1,), (0,)))
        q = q * (1.0 / (SIZES["z"] * SIZES["x"] * SIZES["core"]))
        q_buf[:, cols] = q
        q_hi, q_lo = split(q)
        approx = matmul(o_all, jnp.concatenate([q_hi, q_lo, q_hi], axis=0), ((0,), (0,)))
        r_buf[:, cols] = approx.astype(BF16)
        e_buf[:, cols] = c[:, cols] - approx
        out.append(pltpu.make_async_copy(q_buf.at[:, cols], new_q.at[m, :, cols], sems.at[3 * j]))
        out.append(pltpu.make_async_copy(r_buf.at[:, cols], rebuilt.at[m, :, cols], sems.at[3 * j + 1]))
        out.append(pltpu.make_async_copy(e_buf.at[:, cols], new_errors.at[m, 0, :, cols], sems.at[3 * j + 2]))
        for copy in out[-3:]:
            copy.start()
    for copy in out:
        copy.wait()


def finish(which, raw, factors, c, held=()):
    return pl.pallas_call(
        finish_kernel,
        in_specs=[SCALAR] + in_vmem(3) + anywhere(len(held)),
        out_specs=[pl.BlockSpec(memory_space=pltpu.HBM)] * 3,
        out_shape=[
            jax.ShapeDtypeStruct((2, ROWS, COLS), BF16),
            jax.ShapeDtypeStruct((2, 1, ROWS, COLS), F32),
            jax.ShapeDtypeStruct((2, RANK, COLS), F32),
        ],
        scratch_shapes=[
            pltpu.VMEM((ROWS, COLS), BF16),
            pltpu.VMEM((ROWS, COLS), F32),
            pltpu.VMEM((RANK, COLS), F32),
            pltpu.SemaphoreType.DMA((3 * CHUNKS,)),
        ],
        input_output_aliases={4 + i: i for i in range(len(held))},
        compiler_params=params(),
        cost_estimate=pl.CostEstimate(flops=50_000_000, bytes_accessed=6_000_000, transcendentals=0),
        name="finish_second" if held else "finish_first",
    )(which, raw, factors, c, *held)


def swap(value):
    return lax.ppermute(value, "core", [(0, 1), (1, 0)])


def copies(value, axes):
    count = 1
    for axis in axes:
        count *= SIZES[axis]
    return lax.all_to_all(jnp.broadcast_to(value[None], (count,) + value.shape), axes, 0, 0, tiled=True)


def shards(grads, errors, q_prev):
    core = lax.axis_index("core").astype(jnp.int32)
    c_own, c_oth, left_own, left_oth = correct(core[None], grads, errors, q_prev)
    left_got = swap(left_oth)
    left_got, c_oth = lax.optimization_barrier((left_got, c_oth))
    left = left_own + left_got
    c_got = swap(c_oth)
    left = jnp.sum(copies(left, ("x", "tensor")), axis=0)
    parts = copies(left, ("z",))
    raw, left = right(parts, c_own, c_got)
    factors = factor(left)
    mine = jnp.sum(lax.all_to_all(raw, ("z", "x"), 0, 0, tiled=True), axis=0)
    mine, factors = lax.optimization_barrier((mine, factors))
    factors_got = swap(factors)
    raw = copies(mine, ("z", "x"))
    raw_got = swap(raw)
    outs = finish(core[None], raw, factors, c_own)
    return tuple(finish(1 - core[None], raw_got, factors_got, c_oth, outs))


def solution(mesh):
    fine = Mesh(mesh.devices.reshape(tuple(SIZES.values())), tuple(SIZES))
    dp = ("z", "x", "core")
    in_specs = (
        P(None, dp, None, "tensor"),
        P(None, dp, None, "tensor"),
        P(None, None, "tensor"),
    )
    out_specs = (P(None, None, "tensor"), P(None, dp, None, "tensor"), P(None, None, "tensor"))
    return jax.shard_map(shards, mesh=fine, in_specs=in_specs, out_specs=out_specs, check_vma=False)
```

time: 95.6 us -> 84.7 us (0.89)
  blocking collectives: 60.4 us -> 45.4 us
  waiting for transfers between devices: 3.02 us -> 9.96 us
  starting transfers between devices: 8.74 us -> 13 us
  local copies, waits for them, and re-layouts: 4.74 us -> 1 us
  Pallas kernels: 17.3 us -> 14 us
    all_to_all x1 -> x0, blocking collectives: 15.1 us -> none  [shards(): mine = jnp.sum(lax.all_to_all(raw, ('z', 'x'), 0, 0, tiled=True), axis=0)]
    all_to_all x0 -> x1, waiting for transfers between devices: none -> 9.12 us  [shards(): mine = jnp.sum(lax.all_to_all(raw, ('z', 'x'), 0, 0, tiled=True), axis=0)]
    all_to_all x0 -> x1, starting transfers between devices: none -> 3.88 us  [shards(): mine = jnp.sum(lax.all_to_all(raw, ('z', 'x'), 0, 0, tiled=True), axis=0)]
    unnamed x6 -> x2, local copies, waits for them, and re-layouts: 4.49 us -> 0.75 us
    pallas_call x5, Pallas kernels: 17.3 us -> 14 us  [the longest x2 5.62 us: finish(): pl.pallas_call(finish_kernel, in_specs=[SCALAR] + in_vmem(3) + anywhere(l...]
    ppermute x4, waiting for transfers between devices: 3.02 us -> 0.85 us  [swap(): return lax.ppermute(value, 'core', [(0, 1), (1, 0)])]
  transfers between devices with their start and end apart: 4 -> 5, of which waited for: 1 -> 2; matrix products, arithmetic and copies ran while one was open for 0% -> 0% of each run, Pallas kernels for 7% -> 6%
where the time goes in v2:
time: 84.7 us; the launch traced here: 84.4 us
  blocking collectives  45.4 us (54%)
  Pallas kernels  14 us (17%)
  starting transfers between devices  13 us (15%)
  waiting for transfers between devices  9.96 us (12%)
  local copies, waits for them, and re-layouts  1 us (1%)
    all_to_all x3, blocking collectives, copies(): lax.all_to_all(jnp.broadcast_to(value[None], (count,) + value.shape), axe...  45.4 us
    ppermute x4, starting transfers between devices, swap(): return lax.ppermute(value, 'core', [(0, 1), (1, 0)])  9.15 us
    all_to_all x1, waiting for transfers between devices, shards(): mine = jnp.sum(lax.all_to_all(raw, ('z', 'x'), 0, 0, tiled=True), axis=0)  9.12 us
    pallas_call x2, Pallas kernels, finish(): pl.pallas_call(finish_kernel, in_specs=[SCALAR] + in_vmem(3) + anywhere(l...  5.62 us
    pallas_call x1, Pallas kernels, correct(): pl.pallas_call(correct_kernel, in_specs=[SCALAR] + [pl.BlockSpec(memory_s...  4.9 us
    all_to_all x1, starting transfers between devices, shards(): mine = jnp.sum(lax.all_to_all(raw, ('z', 'x'), 0, 0, tiled=True), axis=0)  3.88 us
    pallas_call x1, Pallas kernels, factor(): pl.pallas_call(factor_kernel, in_specs=in_vmem(1), out_specs=in_vmem(1)[0...  2.98 us
  transfers between devices with their start and end apart: 5, of which 2 were waited for; matrix products, arithmetic and copies ran while one was open for 0% of the time, Pallas kernels for 6%

profile of v2, /device:TPU:1, one launch (start us, length us, event | category | flops | bytes accessed | tf_op | source)
XLA Modules:
  0.0 84.4 jit_solution(2541383731342376713)
XLA Ops:
  0.6 4.9 %correct.1 = (f32[128,3200]{1,0:T(8,128)S(1)}, f32[128,3200]{1,0:T(8,128)}, f32[32,128]{1,0:T(8,128)S(1)}, f32[32,128]{1,0:T(8,128)S(1)}) custom-call(s32[1]{0:T(128)} %bitcast.core_ref.which_ref, bf16[2,1,128,3200]{3,2,1,0:T(8,128)(2,1)} %grads.1, f32[2,1,128,3200]{3,2,1,0:T(8,128)} %errors.1, f32[2,32,3200]{2,1,0:T(8,128)} %q_prev.1), custom_call_target="tpu_custom_call" | custom-call | flops 300000000 | bytes 9000000 | tf_op jit(solution)/shard_map/correct/pallas_call | solution.py:79
  5.5 3.3 %collective-permute-start = (f32[32,128]{1,0:T(8,128)S(1)}, f32[32,128]{1,0:T(8,128)S(1)}, u32[]{:S(2)}, u32[]{:S(2)}) collective-permute-start(f32[32,128]{1,0:T(8,128)S(1)} %get-tuple-element.17), channel_id=1, source_target_pairs={{0,4},{4,0},{1,5},{5,1},{2,6},{6,2},{3,7},{7,3},{8,12},{12,8},{9,1... | collective-permute-start | bytes 49160 | tf_op jit(solution)/shard_map/ppermute | solution.py:218
  8.9 0.8 collective-permute-done
  9.7 0.3 collective-permute-start.1
  10.1 12.6 %all_to_all.20 = f32[16,32,128]{2,1,0:T(8,128)S(1)} all-to-all(f32[16,32,128]{2,1,0:T(8,128)S(1)} %broadcast_in_dim.11), channel_id=1, replica_groups=mesh['z'=8,'x'=4,'core'=2,'tensor'=4] {'x','tensor'}, dimensions={0} | all-to-all | bytes 524288 | tf_op jit(solution)/shard_map/all_to_all | solution.py:225
  22.7 16.0 %all_to_all.21.parts = f32[8,32,128]{2,1,0:T(8,128)S(1)} all-to-all(f32[8,32,128]{2,1,0:T(8,128)S(1)} %broadcast_in_dim.12), channel_id=1, replica_groups=mesh['z'=8,'x'=4,'core'=2,'tensor'=4] {'z'}, dimensions={0} | all-to-all | bytes 262144 | tf_op jit(solution)/shard_map/all_to_all | solution.py:225
  38.7 0.0 collective-permute-done.1.c_got
  38.7 0.5 right_terms.1
  39.2 0.0 copy-start
  39.3 0.7 copy-done
  40.0 3.9 %all-to-all-start.2 = ((f32[32,1,3200]{2,1,0:T(1,128)}), f32[32,1,3200]{2,1,0:T(1,128)S(1)}, u32[]{:S(2)}, u32[]{:S(2)}) async-start(f32[32,1,3200]{2,1,0:T(1,128)} %copy-done), calls=%async_computation.2 | async-start | bytes 819200 | tf_op jit(solution)/shard_map/all_to_all | solution.py:239
  43.9 3.0 %factor.1.factors = f32[2,32,128]{2,1,0:T(8,128)S(1)} custom-call(f32[32,128]{1,0:T(8,128)S(1)} %get-tuple-element.23.left_ref), custom_call_target="tpu_custom_call" | custom-call | flops 10000000 | bytes 10000000 | tf_op jit(solution)/shard_map/factor/pallas_call | solution.py:155
  46.9 9.1 %all-to-all-done.2 = f32[32,1,3200]{2,1,0:T(1,128)S(1)} async-done(((f32[32,1,3200]{2,1,0:T(1,128)}), f32[32,1,3200]{2,1,0:T(1,128)S(1)}, u32[]{:S(2)}, u32[]{:S(2)}) %all-to-all-start.2) | async-done | bytes 409632 | tf_op jit(solution)/shard_map/all_to_all | solution.py:239
  56.0 0.2 reduce_sum.21
  56.3 0.2 broadcast_in_dim.14
  56.5 16.8 %all_to_all.22.raw = f32[32,1,3200]{2,1,0:T(1,128)S(1)} all-to-all(f32[32,1,3200]{2,1,0:T(1,128)S(1)} %broadcast_in_dim.14), channel_id=1, replica_groups=mesh['z'=8,'x'=4,'core'=2,'tensor'=4] {'z','x'}, dimensions={0} | all-to-all | bytes 819200 | tf_op jit(solution)/shard_map/all_to_all | solution.py:225
  73.3 5.5 %collective-permute-start.2 = (f32[32,1,3200]{2,1,0:T(1,128)S(1)}, f32[32,1,3200]{2,1,0:T(1,128)S(1)}, u32[]{:S(2)}, u32[]{:S(2)}) collective-permute-start(f32[32,1,3200]{2,1,0:T(1,128)S(1)} %all_to_all.22.raw), channel_id=1, source_target_pairs={{0,4},{4,0},{1,5},{5,1},{2,6},{6,2},{3,7},{7,3},{8,12},{12,8},{9,1... | collective-permute-start | bytes 1228808 | tf_op jit(solution)/shard_map/ppermute | solution.py:218
  78.7 0.0 collective-permute-start.3
  78.8 2.1 %finish_first.1 = (bf16[2,128,3200]{2,1,0:T(8,128)(2,1)}, f32[2,1,128,3200]{3,2,1,0:T(8,128)}, f32[2,32,3200]{2,1,0:T(8,128)}) custom-call(s32[1]{0:T(128)} %bitcast.core_ref.which_ref, f32[32,1,3200]{2,1,0:T(1,128)S(1)} %all_to_all.22.raw, f32[2,32,128]{2,1,0:T(8,128)S(1)} %factor.1.factors, f32[128,3200]{1,0:T(8,128)S(1)} %get-tuple-element.20.c_own.c), custom_call_target="tpu_custom_call" | custom-call | flops 50000000 | bytes 6000000 | tf_op jit(solution)/shard_map/finish_first/pallas_call | solution.py:195
  80.9 0.0 collective-permute-done.3.factors
  80.9 0.0 collective-permute-done.2.raw
  80.9 3.5 %finish_second.1 = (bf16[2,128,3200]{2,1,0:T(8,128)(2,1)}, f32[2,1,128,3200]{3,2,1,0:T(8,128)}, f32[2,32,3200]{2,1,0:T(8,128)}) custom-call(s32[1]{0:T(128)S(6)} %sub.3.which_ref, f32[32,1,3200]{2,1,0:T(1,128)S(1)} %collective-permute-done.2.raw, ...), custom_call_target="tpu_custom_call", output_to_operand_aliasing={{0}: (4, {}), {1}: (5, {}), {2}: (6, {})} | custom-call | flops 50000000 | bytes 6000000 | tf_op jit(solution)/shard_map/finish_second/pallas_call | solution.py:195
  (6 shorter events, 0.1 us)
Async XLA Ops:
  5.5 4.2 %collective-permute-start = (f32[32,128]{1,0:T(8,128)S(1)}, f32[32,128]{1,0:T(8,128)S(1)}, u32[]{:S(2)}, u32[]{:S(2)}) collective-permute-start(f32[32,128]{1,0:T(8,128)S(1)} %get-tuple-element.17), channel_id=1, source_target_pairs={{0,4},{4,0},{1,5},{5,1},{2,6},{6,2},{3,7},{7,3},{8,12},{12,8},{9,1... | collective-permute-start | bytes 49160 | tf_op jit(solution)/shard_map/ppermute | solution.py:218
  9.7 29.0 %collective-permute-start.1 = (f32[128,3200]{1,0:T(8,128)}, f32[128,3200]{1,0:T(8,128)S(1)}, u32[]{:S(2)}, u32[]{:S(2)}) collective-permute-start(f32[128,3200]{1,0:T(8,128)} %get-tuple-element.21.c), channel_id=1, source_target_pairs={{0,4},{4,0},{1,5},{5,1},{2,6},{6,2},{3,7},{7,3},{8,12},{12,8},{9,1... | collective-permute-start | bytes 4915208 | tf_op jit(solution)/shard_map/ppermute | solution.py:218
  39.2 0.8 copy-start
  40.0 16.0 %all-to-all-start.2 = ((f32[32,1,3200]{2,1,0:T(1,128)}), f32[32,1,3200]{2,1,0:T(1,128)S(1)}, u32[]{:S(2)}, u32[]{:S(2)}) async-start(f32[32,1,3200]{2,1,0:T(1,128)} %copy-done), calls=%async_computation.2 | async-start | bytes 819200 | tf_op jit(solution)/shard_map/all_to_all | solution.py:239
  73.3 7.6 %collective-permute-start.2 = (f32[32,1,3200]{2,1,0:T(1,128)S(1)}, f32[32,1,3200]{2,1,0:T(1,128)S(1)}, u32[]{:S(2)}, u32[]{:S(2)}) collective-permute-start(f32[32,1,3200]{2,1,0:T(1,128)S(1)} %all_to_all.22.raw), channel_id=1, source_target_pairs={{0,4},{4,0},{1,5},{5,1},{2,6},{6,2},{3,7},{7,3},{8,12},{12,8},{9,1... | collective-permute-start | bytes 1228808 | tf_op jit(solution)/shard_map/ppermute | solution.py:218
  78.7 2.1 %collective-permute-start.3 = (f32[2,32,128]{2,1,0:T(8,128)S(1)}, f32[2,32,128]{2,1,0:T(8,128)S(1)}, u32[]{:S(2)}, u32[]{:S(2)}) collective-permute-start(f32[2,32,128]{2,1,0:T(8,128)S(1)} %factor.1.factors), channel_id=1, source_target_pairs={{0,4},{4,0},{1,5},{5,1},{2,6},{6,2},{3,7},{7,3},{8,12},{12,8},{9,1... | collective-permute-start | bytes 98312 | tf_op jit(solution)/shard_map/ppermute | solution.py:218

commit v3 on v2

--- a/solution.py
+++ b/solution.py
@@ -14,6 +14,7 @@
 COLS = 3200
 TILE = 640
 CHUNKS = COLS // TILE
+PIECES = ((0, 1280), (1280, 1920))
 VMEM_BYTES = 24 * 1024 * 1024
 
 
@@ -30,44 +31,63 @@
     return lax.dot_general(a, b, (dims, ((), ())), preferred_element_type=F32)
 
 
-def correct_kernel(core_ref, grads, errors, q_prev, c_own, c_oth, left_own, left_oth, g_buf, q_buf, sems):
+def correct_kernel(core_ref, grads, errors, q_prev, c_own, c_send, left_own, left_oth, c_oth, g_buf, q_buf, sems):
     own = core_ref[0]
-    copies_in = []
-    for slot, (m, c_out) in enumerate(((1 - own, c_oth), (own, c_own))):
-        copies_in.append([pltpu.make_async_copy(q_prev.at[m], q_buf.at[slot], sems.at[slot, 2 * CHUNKS])])
-        for j in range(CHUNKS):
-            cols = pl.ds(j * TILE, TILE)
-            copies_in[slot].append(
+    count = len(PIECES)
+    order = ((1 - own, c_oth, left_oth), (own, c_own, left_own))
+    arrivals = []
+    for slot, (m, c_out, _) in enumerate(order):
+        pieces = []
+        for j, (first, width) in enumerate(PIECES):
+            cols = pl.ds(first, width)
+            pieces.append(
                 (
-                    pltpu.make_async_copy(grads.at[m, 0, :, cols], g_buf.at[slot, j], sems.at[slot, j]),
-                    pltpu.make_async_copy(errors.at[m, 0, :, cols], c_out.at[:, cols], sems.at[slot, CHUNKS + j]),
+                    pltpu.make_async_copy(grads.at[m, 0, :, cols], g_buf.at[slot, :, cols], sems.at[slot, j]),
+                    pltpu.make_async_copy(errors.at[m, 0, :, cols], c_out.at[:, cols], sems.at[slot, count + j]),
                 )
             )
-    for slot in range(2):
-        copies_in[slot][0].start()
-        for g_copy, e_copy in copies_in[slot][1:]:
+        q_copy = pltpu.make_async_copy(q_prev.at[m], q_buf.at[slot], sems.at[slot, 2 * count])
+        arrivals.append((q_copy, pieces))
+    for q_copy, pieces in arrivals:
+        for j, (g_copy, e_copy) in enumerate(pieces):
             g_copy.start()
             e_copy.start()
-    for slot, (c_out, left) in enumerate(((c_oth, left_oth), (c_own, left_own))):
-        copies_in[slot][0].wait()
+            if j == 0:
+                q_copy.start()
+    sends = []
+    for slot, (_, c_out, left) in enumerate(order):
+        q_copy, pieces = arrivals[slot]
         total = jnp.zeros((RANK, ROWS), F32)
-        for j in range(CHUNKS):
-            cols = pl.ds(j * TILE, TILE)
-            for copy in copies_in[slot][1 + j]:
+        for j, (first, width) in enumerate(PIECES):
+            cols = pl.ds(first, width)
+            for copy in pieces[j]:
                 copy.wait()
-            c = g_buf[slot, j].astype(F32) + c_out[:, cols]
+            c = g_buf[slot, :, cols].astype(F32) + c_out[:, cols]
             c_out[:, cols] = c
+            if slot == 0:
+                sends.append(
+                    pltpu.make_async_copy(c_out.at[:, cols], c_send.at[:, cols], sems.at[slot, 2 * count + 1 + j])
+                )
+                sends[-1].start()
+            if j == 0:
+                q_copy.wait()
             c_hi, c_lo = split(c)
             q_hi, q_lo = split(q_buf[slot, :, cols])
             both = matmul(jnp.concatenate([q_hi, q_lo], axis=0), c_hi, ((1,), (1,)))
             total += both[:RANK] + both[RANK:] + matmul(q_hi, c_lo, ((1,), (1,)))
         left[...] = total
+    for copy in sends:
+        copy.wait()
 
 
 def in_vmem(count):
     return [pl.BlockSpec(memory_space=pltpu.VMEM)] * count
 
 
+def in_hbm(count):
+    return [pl.BlockSpec(memory_space=pltpu.HBM)] * count
+
+
 def anywhere(count):
     return [pl.BlockSpec(memory_space=pl.ANY)] * count
 
@@ -78,18 +98,19 @@
 def correct(core, grads, errors, q_prev):
     return pl.pallas_call(
         correct_kernel,
-        in_specs=[SCALAR] + [pl.BlockSpec(memory_space=pltpu.HBM)] * 3,
-        out_specs=in_vmem(4),
+        in_specs=[SCALAR] + in_hbm(3),
+        out_specs=in_vmem(1) + in_hbm(1) + in_vmem(2),
         out_shape=[
-            jax.ShapeDtypeStruct((ROWS, COLS), F32),
-            jax.ShapeDtypeStruct((ROWS, COLS), F32),
+            pltpu.VMEM((ROWS, COLS), F32),
+            pltpu.HBM((ROWS, COLS), F32),
             jax.ShapeDtypeStruct((RANK, ROWS), F32),
             jax.ShapeDtypeStruct((RANK, ROWS), F32),
         ],
         scratch_shapes=[
-            pltpu.VMEM((2, CHUNKS, ROWS, TILE), BF16),
+            pltpu.VMEM((ROWS, COLS), F32),
+            pltpu.VMEM((2, ROWS, COLS), BF16),
             pltpu.VMEM((2, RANK, COLS), F32),
-            pltpu.SemaphoreType.DMA((2, 2 * CHUNKS + 1)),
+            pltpu.SemaphoreType.DMA((2, 3 * len(PIECES) + 1)),
         ],
         compiler_params=params(),
         cost_estimate=pl.CostEstimate(flops=300_000_000, bytes_accessed=9_000_000, transcendentals=0),
@@ -97,28 +118,37 @@
     )(core, *[pltpu.with_memory_space_constraint(x, pltpu.HBM) for x in (grads, errors, q_prev)])
 
 
-def right_kernel(parts, c_own, c_got, raw, left):
+def right_kernel(parts, c_own, c_got, raw, left, raw_buf, sems):
     total = jnp.sum(parts[...], axis=0)
     left[...] = total
     l_hi, l_lo = split(total)
     l_both = jnp.concatenate([l_hi, l_lo], axis=0)
-    for j in range(CHUNKS):
-        cols = pl.ds(j * TILE, TILE)
+    sends = []
+    for j, (first, width) in enumerate(PIECES):
+        cols = pl.ds(first, width)
         s_hi, s_lo = split(c_own[:, cols] + c_got[:, cols])
         both = matmul(l_both, s_hi, ((1,), (0,)))
         value = both[:RANK] + both[RANK:] + matmul(l_hi, s_lo, ((1,), (0,)))
         for k in range(RANK):
-            raw[k, :, cols] = value[k : k + 1]
+            raw_buf[k, :, cols] = value[k : k + 1]
+        sends.append(pltpu.make_async_copy(raw_buf.at[:, :, cols], raw.at[:, :, cols], sems.at[j]))
+        sends[-1].start()
+    for copy in sends:
+        copy.wait()
 
 
 def right(parts, c_own, c_got):
     return pl.pallas_call(
         right_kernel,
         in_specs=in_vmem(3),
-        out_specs=in_vmem(2),
+        out_specs=in_hbm(1) + in_vmem(1),
         out_shape=[
-            jax.ShapeDtypeStruct((RANK, 1, COLS), F32),
+            pltpu.HBM((RANK, 1, COLS), F32),
             jax.ShapeDtypeStruct((RANK, ROWS), F32),
+        ],
+        scratch_shapes=[
+            pltpu.VMEM((RANK, 1, COLS), F32),
+            pltpu.SemaphoreType.DMA((len(PIECES),)),
         ],
         compiler_params=params(),
         cost_estimate=pl.CostEstimate(flops=100_000_000, bytes_accessed=4_000_000, transcendentals=0),
@@ -195,7 +225,7 @@
     return pl.pallas_call(
         finish_kernel,
         in_specs=[SCALAR] + in_vmem(3) + anywhere(len(held)),
-        out_specs=[pl.BlockSpec(memory_space=pltpu.HBM)] * 3,
+        out_specs=in_hbm(3),
         out_shape=[
             jax.ShapeDtypeStruct((2, ROWS, COLS), BF16),
             jax.ShapeDtypeStruct((2, 1, ROWS, COLS), F32),
@@ -236,9 +266,9 @@
     parts = copies(left, ("z",))
     raw, left = right(parts, c_own, c_got)
     factors = factor(left)
+    factors_got = swap(factors)
     mine = jnp.sum(lax.all_to_all(raw, ("z", "x"), 0, 0, tiled=True), axis=0)
-    mine, factors = lax.optimization_barrier((mine, factors))
-    factors_got = swap(factors)
+    mine, factors, factors_got = lax.optimization_barrier((mine, factors, factors_got))
     raw = copies(mine, ("z", "x"))
     raw_got = swap(raw)
     outs = finish(core[None], raw, factors, c_own)

time: 84.7 us -> 82.1 us (0.969)
  starting transfers between devices: 13 us -> 16.1 us
  waiting for transfers between devices: 9.96 us -> 6.92 us
  Pallas kernels: 14 us -> 12 us
    all_to_all x1, waiting for transfers between devices: 9.12 us -> 6.08 us  [shards(): mine = jnp.sum(lax.all_to_all(raw, ('z', 'x'), 0, 0, tiled=True), axis=0)]
    ppermute x4, starting transfers between devices: 9.15 us -> 12.2 us  [swap(): return lax.ppermute(value, 'core', [(0, 1), (1, 0)])]
    pallas_call x2, Pallas kernels: 5.62 us -> 4.19 us  [finish(): pl.pallas_call(finish_kernel, in_specs=[SCALAR] + in_vmem(3) + anywhere(l...]
where the time goes in v3:
time: 82.1 us; the launch traced here: 81.8 us
  blocking collectives  45.5 us (55%)
  starting transfers between devices  16.1 us (20%)
  Pallas kernels  12 us (15%)
  waiting for transfers between devices  6.92 us (8%)
    all_to_all x3, blocking collectives, copies(): lax.all_to_all(jnp.broadcast_to(value[None], (count,) + value.shape), axe...  45.5 us
    ppermute x4, starting transfers between devices, swap(): return lax.ppermute(value, 'core', [(0, 1), (1, 0)])  12.2 us
    all_to_all x1, waiting for transfers between devices, shards(): mine = jnp.sum(lax.all_to_all(raw, ('z', 'x'), 0, 0, tiled=True), axis=0)  6.08 us
    pallas_call x2, Pallas kernels, finish(): pl.pallas_call(finish_kernel, in_specs=[SCALAR] + in_vmem(3) + anywhere(l...  4.19 us
    all_to_all x1, starting transfers between devices, shards(): mine = jnp.sum(lax.all_to_all(raw, ('z', 'x'), 0, 0, tiled=True), axis=0)  3.89 us
    pallas_call x1, Pallas kernels, correct(): pl.pallas_call(correct_kernel, in_specs=[SCALAR] + in_hbm(3), out_specs=i...  3.59 us
    pallas_call x1, Pallas kernels, factor(): pl.pallas_call(factor_kernel, in_specs=in_vmem(1), out_specs=in_vmem(1)[0...  2.98 us
  transfers between devices with their start and end apart: 5, of which 2 were waited for; matrix products, arithmetic and copies ran while one was open for 0% of the time, Pallas kernels for 6%

profile of v3, /device:TPU:1, one launch (start us, length us, event | category | flops | bytes accessed | tf_op | source)
XLA Modules:
  0.0 81.8 jit_solution(3102170702690270670)
XLA Ops:
  0.6 3.6 %correct.1 = (f32[128,3200]{1,0:T(8,128)S(1)}, f32[128,3200]{1,0:T(8,128)}, f32[32,128]{1,0:T(8,128)S(1)}, f32[32,128]{1,0:T(8,128)S(1)}) custom-call(s32[1]{0:T(128)} %bitcast.core_ref.which_ref, bf16[2,1,128,3200]{3,2,1,0:T(8,128)(2,1)} %grads.1, f32[2,1,128,3200]{3,2,1,0:T(8,128)} %errors.1, f32[2,32,3200]{2,1,0:T(8,128)} %q_prev.1), custom_call_target="tpu_custom_call" | custom-call | flops 300000000 | bytes 9000000 | tf_op jit(solution)/shard_map/correct/pallas_call | solution.py:99
  4.2 3.3 %collective-permute-start = (f32[32,128]{1,0:T(8,128)S(1)}, f32[32,128]{1,0:T(8,128)S(1)}, u32[]{:S(2)}, u32[]{:S(2)}) collective-permute-start(f32[32,128]{1,0:T(8,128)S(1)} %get-tuple-element.18), channel_id=1, source_target_pairs={{0,4},{4,0},{1,5},{5,1},{2,6},{6,2},{3,7},{7,3},{8,12},{12,8},{9,1... | collective-permute-start | bytes 49160 | tf_op jit(solution)/shard_map/ppermute | solution.py:248
  7.6 0.8 %collective-permute-done = f32[32,128]{1,0:T(8,128)S(1)} collective-permute-done((f32[32,128]{1,0:T(8,128)S(1)}, f32[32,128]{1,0:T(8,128)S(1)}, u32[]{:S(2)}, u32[]{:S(2)}) %collective-permute-start) | collective-permute-done | bytes 16416 | tf_op jit(solution)/shard_map/ppermute | solution.py:248
  8.4 0.3 collective-permute-start.1
  8.8 12.6 %all_to_all.20 = f32[16,32,128]{2,1,0:T(8,128)S(1)} all-to-all(f32[16,32,128]{2,1,0:T(8,128)S(1)} %broadcast_in_dim.11), channel_id=1, replica_groups=mesh['z'=8,'x'=4,'core'=2,'tensor'=4] {'x','tensor'}, dimensions={0} | all-to-all | bytes 524288 | tf_op jit(solution)/shard_map/all_to_all | solution.py:255
  21.4 16.0 %all_to_all.21.parts = f32[8,32,128]{2,1,0:T(8,128)S(1)} all-to-all(f32[8,32,128]{2,1,0:T(8,128)S(1)} %broadcast_in_dim.12), channel_id=1, replica_groups=mesh['z'=8,'x'=4,'core'=2,'tensor'=4] {'z'}, dimensions={0} | all-to-all | bytes 262144 | tf_op jit(solution)/shard_map/all_to_all | solution.py:255
  37.4 0.0 collective-permute-done.1.c_got
  37.4 1.2 %right_terms.1 = (f32[32,1,3200]{2,1,0:T(1,128)}, f32[32,128]{1,0:T(8,128)S(1)}) custom-call(f32[8,32,128]{2,1,0:T(8,128)S(1)} %all_to_all.21.parts, f32[128,3200]{1,0:T(8,128)S(1)} %get-tuple-element.21.c_own.c, f32[128,3200]{1,0:T(8,128)S(1)} %collective-permute-done.1.c_got), custom_call_target="tpu_custom_call" | custom-call | flops 100000000 | bytes 4000000 | tf_op jit(solution)/shard_map/right_terms/pallas_call | solution.py:141
  38.6 3.9 %all-to-all-start.2 = ((f32[32,1,3200]{2,1,0:T(1,128)}), f32[32,1,3200]{2,1,0:T(1,128)S(1)}, u32[]{:S(2)}, u32[]{:S(2)}) async-start(f32[32,1,3200]{2,1,0:T(1,128)} %get-tuple-element.23), calls=%async_computation.2 | async-start | bytes 819200 | tf_op jit(solution)/shard_map/all_to_all | solution.py:270
  42.5 3.0 %factor.1.factors = f32[2,32,128]{2,1,0:T(8,128)S(1)} custom-call(f32[32,128]{1,0:T(8,128)S(1)} %get-tuple-element.24.left_ref), custom_call_target="tpu_custom_call" | custom-call | flops 10000000 | bytes 10000000 | tf_op jit(solution)/shard_map/factor/pallas_call | solution.py:185
  45.5 3.0 %collective-permute-start.2 = (f32[2,32,128]{2,1,0:T(8,128)S(1)}, f32[2,32,128]{2,1,0:T(8,128)S(1)}, u32[]{:S(2)}, u32[]{:S(2)}) collective-permute-start(f32[2,32,128]{2,1,0:T(8,128)S(1)} %factor.1.factors), channel_id=1, source_target_pairs={{0,4},{4,0},{1,5},{5,1},{2,6},{6,2},{3,7},{7,3},{8,12},{12,8},{9,1... | collective-permute-start | bytes 98312 | tf_op jit(solution)/shard_map/ppermute | solution.py:248
  48.6 6.1 %all-to-all-done.2 = f32[32,1,3200]{2,1,0:T(1,128)S(1)} async-done(((f32[32,1,3200]{2,1,0:T(1,128)}), f32[32,1,3200]{2,1,0:T(1,128)S(1)}, u32[]{:S(2)}, u32[]{:S(2)}) %all-to-all-start.2) | async-done | bytes 409632 | tf_op jit(solution)/shard_map/all_to_all | solution.py:270
  54.6 0.2 reduce_sum.21
  54.9 0.0 collective-permute-done.2.factors
  54.9 0.0 copy-start
  55.0 0.2 broadcast_in_dim.14
  55.2 16.9 %all_to_all.22.raw = f32[32,1,3200]{2,1,0:T(1,128)S(1)} all-to-all(f32[32,1,3200]{2,1,0:T(1,128)S(1)} %broadcast_in_dim.14), channel_id=1, replica_groups=mesh['z'=8,'x'=4,'core'=2,'tensor'=4] {'z','x'}, dimensions={0} | all-to-all | bytes 819200 | tf_op jit(solution)/shard_map/all_to_all | solution.py:255
  72.1 5.5 %collective-permute-start.3 = (f32[32,1,3200]{2,1,0:T(1,128)S(1)}, f32[32,1,3200]{2,1,0:T(1,128)S(1)}, u32[]{:S(2)}, u32[]{:S(2)}) collective-permute-start(f32[32,1,3200]{2,1,0:T(1,128)S(1)} %all_to_all.22.raw), channel_id=1, source_target_pairs={{0,4},{4,0},{1,5},{5,1},{2,6},{6,2},{3,7},{7,3},{8,12},{12,8},{9,1... | collective-permute-start | bytes 1228808 | tf_op jit(solution)/shard_map/ppermute | solution.py:248
  77.5 2.1 %finish_first.1 = (bf16[2,128,3200]{2,1,0:T(8,128)(2,1)}, f32[2,1,128,3200]{3,2,1,0:T(8,128)}, f32[2,32,3200]{2,1,0:T(8,128)}) custom-call(s32[1]{0:T(128)} %bitcast.core_ref.which_ref, f32[32,1,3200]{2,1,0:T(1,128)S(1)} %all_to_all.22.raw, f32[2,32,128]{2,1,0:T(8,128)S(1)} %factor.1.factors, f32[128,3200]{1,0:T(8,128)S(1)} %get-tuple-element.21.c_own.c), custom_call_target="tpu_custom_call" | custom-call | flops 50000000 | bytes 6000000 | tf_op jit(solution)/shard_map/finish_first/pallas_call | solution.py:225
  79.6 0.0 collective-permute-done.3.raw
  79.6 0.0 copy-done
  79.7 2.1 %finish_second.1 = (bf16[2,128,3200]{2,1,0:T(8,128)(2,1)}, f32[2,1,128,3200]{3,2,1,0:T(8,128)}, f32[2,32,3200]{2,1,0:T(8,128)}) custom-call(s32[1]{0:T(128)S(6)} %sub.3.which_ref, f32[32,1,3200]{2,1,0:T(1,128)S(1)} %collective-permute-done.3.raw, ...), custom_call_target="tpu_custom_call", output_to_operand_aliasing={{0}: (4, {}), {1}: (5, {}), {2}: (6, {})} | custom-call | flops 50000000 | bytes 6000000 | tf_op jit(solution)/shard_map/finish_second/pallas_call | solution.py:225
  (6 shorter events, 0.1 us)
Async XLA Ops:
  4.2 4.2 %collective-permute-start = (f32[32,128]{1,0:T(8,128)S(1)}, f32[32,128]{1,0:T(8,128)S(1)}, u32[]{:S(2)}, u32[]{:S(2)}) collective-permute-start(f32[32,128]{1,0:T(8,128)S(1)} %get-tuple-element.18), channel_id=1, source_target_pairs={{0,4},{4,0},{1,5},{5,1},{2,6},{6,2},{3,7},{7,3},{8,12},{12,8},{9,1... | collective-permute-start | bytes 49160 | tf_op jit(solution)/shard_map/ppermute | solution.py:248
  8.4 29.0 %collective-permute-start.1 = (f32[128,3200]{1,0:T(8,128)}, f32[128,3200]{1,0:T(8,128)S(1)}, u32[]{:S(2)}, u32[]{:S(2)}) collective-permute-start(f32[128,3200]{1,0:T(8,128)} %get-tuple-element.22.c), channel_id=1, source_target_pairs={{0,4},{4,0},{1,5},{5,1},{2,6},{6,2},{3,7},{7,3},{8,12},{12,8},{9,1... | collective-permute-start | bytes 4915208 | tf_op jit(solution)/shard_map/ppermute | solution.py:248
  38.6 16.0 %all-to-all-start.2 = ((f32[32,1,3200]{2,1,0:T(1,128)}), f32[32,1,3200]{2,1,0:T(1,128)S(1)}, u32[]{:S(2)}, u32[]{:S(2)}) async-start(f32[32,1,3200]{2,1,0:T(1,128)} %get-tuple-element.23), calls=%async_computation.2 | async-start | bytes 819200 | tf_op jit(solution)/shard_map/all_to_all | solution.py:270
  45.5 9.4 %collective-permute-start.2 = (f32[2,32,128]{2,1,0:T(8,128)S(1)}, f32[2,32,128]{2,1,0:T(8,128)S(1)}, u32[]{:S(2)}, u32[]{:S(2)}) collective-permute-start(f32[2,32,128]{2,1,0:T(8,128)S(1)} %factor.1.factors), channel_id=1, source_target_pairs={{0,4},{4,0},{1,5},{5,1},{2,6},{6,2},{3,7},{7,3},{8,12},{12,8},{9,1... | collective-permute-start | bytes 98312 | tf_op jit(solution)/shard_map/ppermute | solution.py:248
  54.9 24.7 %copy-start = (f32[128,3200]{1,0:T(8,128)S(1)}, f32[128,3200]{1,0:T(8,128)}, u32[]{:S(2)}) copy-start(f32[128,3200]{1,0:T(8,128)} %get-tuple-element.22.c) | copy-start | bytes 4915204
  72.1 7.6 %collective-permute-start.3 = (f32[32,1,3200]{2,1,0:T(1,128)S(1)}, f32[32,1,3200]{2,1,0:T(1,128)S(1)}, u32[]{:S(2)}, u32[]{:S(2)}) collective-permute-start(f32[32,1,3200]{2,1,0:T(1,128)S(1)} %all_to_all.22.raw), channel_id=1, source_target_pairs={{0,4},{4,0},{1,5},{5,1},{2,6},{6,2},{3,7},{7,3},{8,12},{12,8},{9,1... | collective-permute-start | bytes 1228808 | tf_op jit(solution)/shard_map/ppermute | solution.py:248

commit v4 on v3

--- a/solution.py
+++ b/solution.py
@@ -12,9 +12,8 @@
 RANK = 32
 ROWS = 128
 COLS = 3200
-TILE = 640
-CHUNKS = COLS // TILE
 PIECES = ((0, 1280), (1280, 1920))
+OUT_PIECES = ((0, 640), (640, 1280), (1920, 1280))
 VMEM_BYTES = 24 * 1024 * 1024
 
 
@@ -118,37 +117,28 @@
     )(core, *[pltpu.with_memory_space_constraint(x, pltpu.HBM) for x in (grads, errors, q_prev)])
 
 
-def right_kernel(parts, c_own, c_got, raw, left, raw_buf, sems):
+def right_kernel(parts, c_own, c_got, raw, left):
     total = jnp.sum(parts[...], axis=0)
     left[...] = total
     l_hi, l_lo = split(total)
     l_both = jnp.concatenate([l_hi, l_lo], axis=0)
-    sends = []
-    for j, (first, width) in enumerate(PIECES):
+    for first, width in PIECES:
         cols = pl.ds(first, width)
         s_hi, s_lo = split(c_own[:, cols] + c_got[:, cols])
         both = matmul(l_both, s_hi, ((1,), (0,)))
         value = both[:RANK] + both[RANK:] + matmul(l_hi, s_lo, ((1,), (0,)))
         for k in range(RANK):
-            raw_buf[k, :, cols] = value[k : k + 1]
-        sends.append(pltpu.make_async_copy(raw_buf.at[:, :, cols], raw.at[:, :, cols], sems.at[j]))
-        sends[-1].start()
-    for copy in sends:
-        copy.wait()
+            raw[k, :, cols] = value[k : k + 1]
 
 
 def right(parts, c_own, c_got):
     return pl.pallas_call(
         right_kernel,
         in_specs=in_vmem(3),
-        out_specs=in_hbm(1) + in_vmem(1),
+        out_specs=in_vmem(2),
         out_shape=[
-            pltpu.HBM((RANK, 1, COLS), F32),
+            jax.ShapeDtypeStruct((RANK, 1, COLS), F32),
             jax.ShapeDtypeStruct((RANK, ROWS), F32),
-        ],
-        scratch_shapes=[
-            pltpu.VMEM((RANK, 1, COLS), F32),
-            pltpu.SemaphoreType.DMA((len(PIECES),)),
         ],
         compiler_params=params(),
         cost_estimate=pl.CostEstimate(flops=100_000_000, bytes_accessed=4_000_000, transcendentals=0),
@@ -177,8 +167,12 @@
     ortho = lax.dot_general(
         inverse, left, (((1,), (0,)), ((), ())), precision=lax.Precision.HIGHEST, preferred_element_type=F32
     )
-    out[0] = ortho
-    out[1] = jnp.concatenate([inverse, jnp.zeros((RANK, ROWS - RANK), F32)], axis=1)
+    twice = lax.dot_general(
+        inverse, ortho, (((0,), (0,)), ((), ())), precision=lax.Precision.HIGHEST, preferred_element_type=F32
+    )
+    share = 1.0 / (SIZES["z"] * SIZES["x"] * SIZES["core"])
+    out[0] = twice * share
+    out[1] = jnp.concatenate([inverse.T * share, jnp.zeros((RANK, ROWS - RANK), F32)], axis=1)
 
 
 def factor(left):
@@ -196,27 +190,24 @@
 def finish_kernel(which_ref, raw, factors, c, *refs):
     rebuilt, new_errors, new_q, r_buf, e_buf, q_buf, sems = refs[-7:]
     m = which_ref[0]
-    i_hi, i_lo = split(factors[1][:, :RANK])
-    i_all = jnp.concatenate([i_hi, i_hi, i_lo], axis=1)
-    o_hi, o_lo = split(factors[0])
-    o_all = jnp.concatenate([o_hi, o_hi, o_lo], axis=0)
+    f_hi, f_lo = split(jnp.concatenate([factors[0], factors[1][:, :RANK]], axis=1))
+    f_all = jnp.concatenate([f_hi, f_hi, f_lo], axis=0)
     out = []
-    for j in range(CHUNKS):
-        cols = pl.ds(j * TILE, TILE)
+    for j, (first, width) in enumerate(OUT_PIECES):
+        cols = pl.ds(first, width)
         rows = jnp.concatenate([raw[k, :, cols] for k in range(RANK)], axis=0)
         r_hi, r_lo = split(rows)
-        q = matmul(i_all, jnp.concatenate([r_hi, r_lo, r_hi], axis=0), ((1,), (0,)))
-        q = q * (1.0 / (SIZES["z"] * SIZES["x"] * SIZES["core"]))
-        q_buf[:, cols] = q
-        q_hi, q_lo = split(q)
-        approx = matmul(o_all, jnp.concatenate([q_hi, q_lo, q_hi], axis=0), ((0,), (0,)))
+        both = matmul(f_all, jnp.concatenate([r_hi, r_lo, r_hi], axis=0), ((0,), (0,)))
+        approx = both[:ROWS]
+        e_buf[:, cols] = c[:, cols] - approx
+        out.append(pltpu.make_async_copy(e_buf.at[:, cols], new_errors.at[m, 0, :, cols], sems.at[3 * j]))
+        out[-1].start()
         r_buf[:, cols] = approx.astype(BF16)
-        e_buf[:, cols] = c[:, cols] - approx
-        out.append(pltpu.make_async_copy(q_buf.at[:, cols], new_q.at[m, :, cols], sems.at[3 * j]))
         out.append(pltpu.make_async_copy(r_buf.at[:, cols], rebuilt.at[m, :, cols], sems.at[3 * j + 1]))
-        out.append(pltpu.make_async_copy(e_buf.at[:, cols], new_errors.at[m, 0, :, cols], sems.at[3 * j + 2]))
-        for copy in out[-3:]:
-            copy.start()
+        out[-1].start()
+        q_buf[:, cols] = both[ROWS:]
+        out.append(pltpu.make_async_copy(q_buf.at[:, cols], new_q.at[m, :, cols], sems.at[3 * j + 2]))
+        out[-1].start()
     for copy in out:
         copy.wait()
 
@@ -235,7 +226,7 @@
             pltpu.VMEM((ROWS, COLS), BF16),
             pltpu.VMEM((ROWS, COLS), F32),
             pltpu.VMEM((RANK, COLS), F32),
-            pltpu.SemaphoreType.DMA((3 * CHUNKS,)),
+            pltpu.SemaphoreType.DMA((3 * len(OUT_PIECES),)),
         ],
         input_output_aliases={4 + i: i for i in range(len(held))},
         compiler_params=params(),
@@ -265,11 +256,12 @@
     left = jnp.sum(copies(left, ("x", "tensor")), axis=0)
     parts = copies(left, ("z",))
     raw, left = right(parts, c_own, c_got)
+    mine = jnp.sum(lax.all_to_all(raw, ("z", "x"), 0, 0, tiled=True), axis=0)
+    mine, left = lax.optimization_barrier((mine, left))
     factors = factor(left)
     factors_got = swap(factors)
-    mine = jnp.sum(lax.all_to_all(raw, ("z", "x"), 0, 0, tiled=True), axis=0)
-    mine, factors, factors_got = lax.optimization_barrier((mine, factors, factors_got))
     raw = copies(mine, ("z", "x"))
+    raw, factors, factors_got = lax.optimization_barrier((raw, factors, factors_got))
     raw_got = swap(raw)
     outs = finish(core[None], raw, factors, c_own)
     return tuple(finish(1 - core[None], raw_got, factors_got, c_oth, outs))

time: 82.1 us -> 80.8 us (0.984)
  blocking collectives: 45.5 us -> 43.7 us
  starting transfers between devices: 16.1 us -> 17.9 us
  waiting for transfers between devices: 6.92 us -> 5.84 us
  Pallas kernels: 12 us -> 11 us
    all_to_all x3 -> x2, blocking collectives: 45.5 us -> 28.6 us  [copies(): lax.all_to_all(jnp.broadcast_to(value[None], (count,) + value.shape), axe...]
    all_to_all x0 -> x1, blocking collectives: none -> 15.1 us  [shards(): mine = jnp.sum(lax.all_to_all(raw, ('z', 'x'), 0, 0, tiled=True), axis=0)]
    all_to_all x1, waiting for transfers between devices: 6.08 us -> 4.14 us  [copies(): lax.all_to_all(jnp.broadcast_to(value[None], (count,) + value.shape), axe...]
    all_to_all x1, starting transfers between devices: 3.89 us -> 5.35 us  [copies(): lax.all_to_all(jnp.broadcast_to(value[None], (count,) + value.shape), axe...]
    ppermute x4, waiting for transfers between devices: 0.85 us -> 1.7 us  [swap(): return lax.ppermute(value, 'core', [(0, 1), (1, 0)])]
  transfers between devices with their start and end apart: 5 -> 5, of which waited for: 2 -> 3; matrix products, arithmetic and copies ran while one was open for 0% -> 0% of each run, Pallas kernels for 6% -> 6%
where the time goes in v4:
time: 80.8 us; the launch traced here: 80.5 us
  blocking collectives  43.7 us (54%)
  starting transfers between devices  17.9 us (22%)
  Pallas kernels  11 us (14%)
  waiting for transfers between devices  5.84 us (7%)
  local copies, waits for them, and re-layouts  1.01 us (1%)
    all_to_all x2, blocking collectives, copies(): lax.all_to_all(jnp.broadcast_to(value[None], (count,) + value.shape), axe...  28.6 us
    all_to_all x1, blocking collectives, shards(): mine = jnp.sum(lax.all_to_all(raw, ('z', 'x'), 0, 0, tiled=True), axis=0)  15.1 us
    ppermute x4, starting transfers between devices, swap(): return lax.ppermute(value, 'core', [(0, 1), (1, 0)])  12.6 us
    all_to_all x1, starting transfers between devices, copies(): lax.all_to_all(jnp.broadcast_to(value[None], (count,) + value.shape), axe...  5.35 us
    all_to_all x1, waiting for transfers between devices, copies(): lax.all_to_all(jnp.broadcast_to(value[None], (count,) + value.shape), axe...  4.14 us
    pallas_call x2, Pallas kernels, finish(): pl.pallas_call(finish_kernel, in_specs=[SCALAR] + in_vmem(3) + anywhere(l...  3.77 us
    pallas_call x1, Pallas kernels, correct(): pl.pallas_call(correct_kernel, in_specs=[SCALAR] + in_hbm(3), out_specs=i...  3.59 us
    pallas_call x1, Pallas kernels, factor(): pl.pallas_call(factor_kernel, in_specs=in_vmem(1), out_specs=in_vmem(1)[0...  3.15 us
  transfers between devices with their start and end apart: 5, of which 3 were waited for; matrix products, arithmetic and copies ran while one was open for 0% of the time, Pallas kernels for 6%

profile of v4, /device:TPU:1, one launch (start us, length us, event | category | flops | bytes accessed | tf_op | source)
XLA Modules:
  0.0 80.5 jit_solution(17236835844041087513)
XLA Ops:
  0.6 3.6 %correct.1 = (f32[128,3200]{1,0:T(8,128)S(1)}, f32[128,3200]{1,0:T(8,128)}, f32[32,128]{1,0:T(8,128)S(1)}, f32[32,128]{1,0:T(8,128)S(1)}) custom-call(s32[1]{0:T(128)} %bitcast.core_ref.which_ref, bf16[2,1,128,3200]{3,2,1,0:T(8,128)(2,1)} %grads.1, f32[2,1,128,3200]{3,2,1,0:T(8,128)} %errors.1, f32[2,32,3200]{2,1,0:T(8,128)} %q_prev.1), custom_call_target="tpu_custom_call" | custom-call | flops 300000000 | bytes 9000000 | tf_op jit(solution)/shard_map/correct/pallas_call | solution.py:98
  4.2 3.3 %collective-permute-start = (f32[32,128]{1,0:T(8,128)S(1)}, f32[32,128]{1,0:T(8,128)S(1)}, u32[]{:S(2)}, u32[]{:S(2)}) collective-permute-start(f32[32,128]{1,0:T(8,128)S(1)} %get-tuple-element.20), channel_id=1, source_target_pairs={{0,4},{4,0},{1,5},{5,1},{2,6},{6,2},{3,7},{7,3},{8,12},{12,8},{9,1... | collective-permute-start | bytes 49160 | tf_op jit(solution)/shard_map/ppermute | solution.py:239
  7.6 0.8 %collective-permute-done = f32[32,128]{1,0:T(8,128)S(1)} collective-permute-done((f32[32,128]{1,0:T(8,128)S(1)}, f32[32,128]{1,0:T(8,128)S(1)}, u32[]{:S(2)}, u32[]{:S(2)}) %collective-permute-start) | collective-permute-done | bytes 16416 | tf_op jit(solution)/shard_map/ppermute | solution.py:239
  8.4 0.3 collective-permute-start.1
  8.8 12.6 %all_to_all.20 = f32[16,32,128]{2,1,0:T(8,128)S(1)} all-to-all(f32[16,32,128]{2,1,0:T(8,128)S(1)} %broadcast_in_dim.11), channel_id=1, replica_groups=mesh['z'=8,'x'=4,'core'=2,'tensor'=4] {'x','tensor'}, dimensions={0} | all-to-all | bytes 524288 | tf_op jit(solution)/shard_map/all_to_all | solution.py:246
  21.4 16.0 %all_to_all.21.parts = f32[8,32,128]{2,1,0:T(8,128)S(1)} all-to-all(f32[8,32,128]{2,1,0:T(8,128)S(1)} %broadcast_in_dim.12), channel_id=1, replica_groups=mesh['z'=8,'x'=4,'core'=2,'tensor'=4] {'z'}, dimensions={0} | all-to-all | bytes 262144 | tf_op jit(solution)/shard_map/all_to_all | solution.py:246
  37.4 0.0 collective-permute-done.1.c_got
  37.4 0.5 right_terms.1
  37.9 15.1 %all_to_all.22 = f32[32,1,3200]{2,1,0:T(1,128)S(1)} all-to-all(f32[32,1,3200]{2,1,0:T(1,128)S(1)} %get-tuple-element.25), channel_id=1, replica_groups=mesh['z'=8,'x'=4,'core'=2,'tensor'=4] {'z','x'}, dimensions={0} | all-to-all | bytes 819200 | tf_op jit(solution)/shard_map/all_to_all | solution.py:259
  53.0 0.2 reduce_sum.21
  53.3 1.0 %broadcast_in_dim.14 = f32[32,1,3200]{2,1,0:T(1,128)} broadcast(f32[3200]{0:T(1024)S(1)} %reduce.1), dimensions={2} | broadcast | bytes 422400 | tf_op jit(solution)/shard_map/broadcast_in_dim | solution.py:246
  54.3 5.4 %all-to-all-start.3 = ((f32[32,1,3200]{2,1,0:T(1,128)}), f32[32,1,3200]{2,1,0:T(1,128)S(1)}, u32[]{:S(2)}, u32[]{:S(2)}) async-start(f32[32,1,3200]{2,1,0:T(1,128)} %broadcast_in_dim.14), calls=%async_computation.3 | async-start | bytes 819200 | tf_op jit(solution)/shard_map/all_to_all | solution.py:246
  59.6 3.1 %factor.1.factors = f32[2,32,128]{2,1,0:T(8,128)S(1)} custom-call(f32[32,128]{1,0:T(8,128)S(1)} %get-tuple-element.28.left_ref), custom_call_target="tpu_custom_call" | custom-call | flops 10000000 | bytes 10000000 | tf_op jit(solution)/shard_map/factor/pallas_call | solution.py:179
  62.8 3.5 %collective-permute-start.2 = (f32[2,32,128]{2,1,0:T(8,128)S(1)}, f32[2,32,128]{2,1,0:T(8,128)S(1)}, u32[]{:S(2)}, u32[]{:S(2)}) collective-permute-start(f32[2,32,128]{2,1,0:T(8,128)S(1)} %factor.1.factors), channel_id=1, source_target_pairs={{0,4},{4,0},{1,5},{5,1},{2,6},{6,2},{3,7},{7,3},{8,12},{12,8},{9,1... | collective-permute-start | bytes 98312 | tf_op jit(solution)/shard_map/ppermute | solution.py:239
  66.2 0.9 %collective-permute-done.2.factors = f32[2,32,128]{2,1,0:T(8,128)S(1)} collective-permute-done((f32[2,32,128]{2,1,0:T(8,128)S(1)}, f32[2,32,128]{2,1,0:T(8,128)S(1)}, u32[]{:S(2)}, u32[]{:S(2)}) %collective-permute-start.2) | collective-permute-done | bytes 32800 | tf_op jit(solution)/shard_map/ppermute | solution.py:239
  67.1 4.1 %all-to-all-done.3.raw = f32[32,1,3200]{2,1,0:T(1,128)S(1)} async-done(((f32[32,1,3200]{2,1,0:T(1,128)}), f32[32,1,3200]{2,1,0:T(1,128)S(1)}, u32[]{:S(2)}, u32[]{:S(2)}) %all-to-all-start.3) | async-done | bytes 409632 | tf_op jit(solution)/shard_map/all_to_all | solution.py:246
  71.2 0.0 copy-start
  71.2 5.5 %collective-permute-start.3 = (f32[32,1,3200]{2,1,0:T(1,128)S(1)}, f32[32,1,3200]{2,1,0:T(1,128)S(1)}, u32[]{:S(2)}, u32[]{:S(2)}) collective-permute-start(f32[32,1,3200]{2,1,0:T(1,128)S(1)} %all-to-all-done.3.raw), channel_id=1, source_target_pairs={{0,4},{4,0},{1,5},{5,1},{2,6},{6,2},{3,7},{7,3},{8,12},{12,8},{9,1... | collective-permute-start | bytes 1228808 | tf_op jit(solution)/shard_map/ppermute | solution.py:239
  76.7 1.9 %finish_first.1 = (bf16[2,128,3200]{2,1,0:T(8,128)(2,1)}, f32[2,1,128,3200]{3,2,1,0:T(8,128)}, f32[2,32,3200]{2,1,0:T(8,128)}) custom-call(s32[1]{0:T(128)} %bitcast.core_ref.which_ref, f32[32,1,3200]{2,1,0:T(1,128)S(1)} %all-to-all-done.3.raw, f32[2,32,128]{2,1,0:T(8,128)S(1)} %factor.1.factors, f32[128,3200]{1,0:T(8,128)S(1)} %get-tuple-element.23.c_own.c), custom_call_target="tpu_custom_call" | custom-call | flops 50000000 | bytes 6000000 | tf_op jit(solution)/shard_map/finish_first/pallas_call | solution.py:216
  78.6 0.0 collective-permute-done.3.raw
  78.6 0.0 copy-done
  78.6 1.9 %finish_second.1 = (bf16[2,128,3200]{2,1,0:T(8,128)(2,1)}, f32[2,1,128,3200]{3,2,1,0:T(8,128)}, f32[2,32,3200]{2,1,0:T(8,128)}) custom-call(s32[1]{0:T(128)S(6)} %sub.3.which_ref, f32[32,1,3200]{2,1,0:T(1,128)S(1)} %collective-permute-done.3.raw, ...), custom_call_target="tpu_custom_call", output_to_operand_aliasing={{0}: (4, {}), {1}: (5, {}), {2}: (6, {})} | custom-call | flops 50000000 | bytes 6000000 | tf_op jit(solution)/shard_map/finish_second/pallas_call | solution.py:216
  (6 shorter events, 0.1 us)
Async XLA Ops:
  4.2 4.2 %collective-permute-start = (f32[32,128]{1,0:T(8,128)S(1)}, f32[32,128]{1,0:T(8,128)S(1)}, u32[]{:S(2)}, u32[]{:S(2)}) collective-permute-start(f32[32,128]{1,0:T(8,128)S(1)} %get-tuple-element.20), channel_id=1, source_target_pairs={{0,4},{4,0},{1,5},{5,1},{2,6},{6,2},{3,7},{7,3},{8,12},{12,8},{9,1... | collective-permute-start | bytes 49160 | tf_op jit(solution)/shard_map/ppermute | solution.py:239
  8.4 29.0 %collective-permute-start.1 = (f32[128,3200]{1,0:T(8,128)}, f32[128,3200]{1,0:T(8,128)S(1)}, u32[]{:S(2)}, u32[]{:S(2)}) collective-permute-start(f32[128,3200]{1,0:T(8,128)} %get-tuple-element.24.c), channel_id=1, source_target_pairs={{0,4},{4,0},{1,5},{5,1},{2,6},{6,2},{3,7},{7,3},{8,12},{12,8},{9,1... | collective-permute-start | bytes 4915208 | tf_op jit(solution)/shard_map/ppermute | solution.py:239
  54.3 17.0 %all-to-all-start.3 = ((f32[32,1,3200]{2,1,0:T(1,128)}), f32[32,1,3200]{2,1,0:T(1,128)S(1)}, u32[]{:S(2)}, u32[]{:S(2)}) async-start(f32[32,1,3200]{2,1,0:T(1,128)} %broadcast_in_dim.14), calls=%async_computation.3 | async-start | bytes 819200 | tf_op jit(solution)/shard_map/all_to_all | solution.py:246
  62.8 4.3 %collective-permute-start.2 = (f32[2,32,128]{2,1,0:T(8,128)S(1)}, f32[2,32,128]{2,1,0:T(8,128)S(1)}, u32[]{:S(2)}, u32[]{:S(2)}) collective-permute-start(f32[2,32,128]{2,1,0:T(8,128)S(1)} %factor.1.factors), channel_id=1, source_target_pairs={{0,4},{4,0},{1,5},{5,1},{2,6},{6,2},{3,7},{7,3},{8,12},{12,8},{9,1... | collective-permute-start | bytes 98312 | tf_op jit(solution)/shard_map/ppermute | solution.py:239
  71.2 7.4 %copy-start = (f32[128,3200]{1,0:T(8,128)S(1)}, f32[128,3200]{1,0:T(8,128)}, u32[]{:S(2)}) copy-start(f32[128,3200]{1,0:T(8,128)} %get-tuple-element.24.c) | copy-start | bytes 4915204
  71.2 7.4 %collective-permute-start.3 = (f32[32,1,3200]{2,1,0:T(1,128)S(1)}, f32[32,1,3200]{2,1,0:T(1,128)S(1)}, u32[]{:S(2)}, u32[]{:S(2)}) collective-permute-start(f32[32,1,3200]{2,1,0:T(1,128)S(1)} %all-to-all-done.3.raw), channel_id=1, source_target_pairs={{0,4},{4,0},{1,5},{5,1},{2,6},{6,2},{3,7},{7,3},{8,12},{12,8},{9,1... | collective-permute-start | bytes 1228808 | tf_op jit(solution)/shard_map/ppermute | solution.py:239

commit v5 on v4

--- a/solution.py
+++ b/solution.py
@@ -13,6 +13,7 @@
 ROWS = 128
 COLS = 3200
 PIECES = ((0, 1280), (1280, 1920))
+GROUPS = 4
 OUT_PIECES = ((0, 640), (640, 1280), (1920, 1280))
 VMEM_BYTES = 24 * 1024 * 1024
 
@@ -30,53 +31,67 @@
     return lax.dot_general(a, b, (dims, ((), ())), preferred_element_type=F32)
 
 
-def correct_kernel(core_ref, grads, errors, q_prev, c_own, c_send, left_own, left_oth, c_oth, g_buf, q_buf, sems):
+def left_terms(c, q):
+    c_hi, c_lo = split(c)
+    q_hi, q_lo = split(q)
+    both = matmul(jnp.concatenate([q_hi, q_lo], axis=0), c_hi, ((1,), (1,)))
+    return both[:RANK] + both[RANK:] + matmul(q_hi, c_lo, ((1,), (1,)))
+
+
+def other_kernel(
+    core_ref, grads, errors, q_prev, c_oth, left, g_own, e_own, q_own, g_oth, q_oth, sems, own_sems
+):
     own = core_ref[0]
+    oth = 1 - own
     count = len(PIECES)
-    order = ((1 - own, c_oth, left_oth), (own, c_own, left_own))
     arrivals = []
-    for slot, (m, c_out, _) in enumerate(order):
-        pieces = []
-        for j, (first, width) in enumerate(PIECES):
-            cols = pl.ds(first, width)
-            pieces.append(
-                (
-                    pltpu.make_async_copy(grads.at[m, 0, :, cols], g_buf.at[slot, :, cols], sems.at[slot, j]),
-                    pltpu.make_async_copy(errors.at[m, 0, :, cols], c_out.at[:, cols], sems.at[slot, count + j]),
-                )
+    for j, (first, width) in enumerate(PIECES):
+        cols = pl.ds(first, width)
+        arrivals.append(
+            (
+                pltpu.make_async_copy(grads.at[oth, 0, :, cols], g_oth.at[:, cols], sems.at[j]),
+                pltpu.make_async_copy(errors.at[oth, 0, :, cols], c_oth.at[:, cols], sems.at[count + j]),
             )
-        q_copy = pltpu.make_async_copy(q_prev.at[m], q_buf.at[slot], sems.at[slot, 2 * count])
-        arrivals.append((q_copy, pieces))
-    for q_copy, pieces in arrivals:
-        for j, (g_copy, e_copy) in enumerate(pieces):
-            g_copy.start()
-            e_copy.start()
-            if j == 0:
-                q_copy.start()
-    sends = []
-    for slot, (_, c_out, left) in enumerate(order):
-        q_copy, pieces = arrivals[slot]
-        total = jnp.zeros((RANK, ROWS), F32)
-        for j, (first, width) in enumerate(PIECES):
-            cols = pl.ds(first, width)
-            for copy in pieces[j]:
-                copy.wait()
-            c = g_buf[slot, :, cols].astype(F32) + c_out[:, cols]
-            c_out[:, cols] = c
-            if slot == 0:
-                sends.append(
-                    pltpu.make_async_copy(c_out.at[:, cols], c_send.at[:, cols], sems.at[slot, 2 * count + 1 + j])
-                )
-                sends[-1].start()
-            if j == 0:
-                q_copy.wait()
-            c_hi, c_lo = split(c)
-            q_hi, q_lo = split(q_buf[slot, :, cols])
-            both = matmul(jnp.concatenate([q_hi, q_lo], axis=0), c_hi, ((1,), (1,)))
-            total += both[:RANK] + both[RANK:] + matmul(q_hi, c_lo, ((1,), (1,)))
-        left[...] = total
-    for copy in sends:
+        )
+    q_copy = pltpu.make_async_copy(q_prev.at[oth], q_oth, sems.at[2 * count])
+    keeps = (
+        pltpu.make_async_copy(grads.at[own, 0], g_own, own_sems.at[0]),
+        pltpu.make_async_copy(errors.at[own, 0], e_own, own_sems.at[1]),
+        pltpu.make_async_copy(q_prev.at[own], q_own, own_sems.at[2]),
+    )
+    for j, pair in enumerate(arrivals):
+        for copy in pair:
+            copy.start()
+        if j == 0:
+            q_copy.start()
+    for copy in keeps:
+        copy.start()
+    total = jnp.zeros((RANK, ROWS), F32)
+    for j, (first, width) in enumerate(PIECES):
+        cols = pl.ds(first, width)
+        for copy in arrivals[j]:
+            copy.wait()
+        c = g_oth[:, cols].astype(F32) + c_oth[:, cols]
+        c_oth[:, cols] = c
+        if j == 0:
+            q_copy.wait()
+        total += left_terms(c, q_oth[:, cols])
+    left[...] = total
+    for copy in keeps:
         copy.wait()
+
+
+def own_kernel(g, e, q, c_oth, c_out, left, c_send, sem):
+    send = pltpu.make_async_copy(c_oth, c_send, sem)
+    send.start()
+    total = jnp.zeros((RANK, ROWS), F32)
+    for first, width in PIECES:
+        cols = pl.ds(first, width)
+        c = g[:, cols].astype(F32) + e[:, cols]
+        c_out[:, cols] = c
+        total += left_terms(c, q[:, cols])
+    left[...] = total
+    send.wait()
 
 
 def in_vmem(count):
@@ -94,27 +109,41 @@
 SCALAR = pl.BlockSpec(memory_space=pltpu.SMEM)
 
 
-def correct(core, grads, errors, q_prev):
-    return pl.pallas_call(
-        correct_kernel,
+def correct_other(core, grads, errors, q_prev):
+    return pl.pallas_call(
+        other_kernel,
         in_specs=[SCALAR] + in_hbm(3),
-        out_specs=in_vmem(1) + in_hbm(1) + in_vmem(2),
+        out_specs=in_vmem(5),
         out_shape=[
             pltpu.VMEM((ROWS, COLS), F32),
-            pltpu.HBM((ROWS, COLS), F32),
-            jax.ShapeDtypeStruct((RANK, ROWS), F32),
-            jax.ShapeDtypeStruct((RANK, ROWS), F32),
+            pltpu.VMEM((RANK, ROWS), F32),
+            pltpu.VMEM((ROWS, COLS), BF16),
+            pltpu.VMEM((ROWS, COLS), F32),
+            pltpu.VMEM((RANK, COLS), F32),
         ],
         scratch_shapes=[
-            pltpu.VMEM((ROWS, COLS), F32),
-            pltpu.VMEM((2, ROWS, COLS), BF16),
-            pltpu.VMEM((2, RANK, COLS), F32),
-            pltpu.SemaphoreType.DMA((2, 3 * len(PIECES) + 1)),
-        ],
-        compiler_params=params(),
-        cost_estimate=pl.CostEstimate(flops=300_000_000, bytes_accessed=9_000_000, transcendentals=0),
-        name="correct",
+            pltpu.VMEM((ROWS, COLS), BF16),
+            pltpu.VMEM((RANK, COLS), F32),
+            pltpu.SemaphoreType.DMA((2 * len(PIECES) + 1,)),
+            pltpu.SemaphoreType.DMA((3,)),
+        ],
+        compiler_params=params(),
+        cost_estimate=pl.CostEstimate(flops=150_000_000, bytes_accessed=9_000_000, transcendentals=0),
+        name="correct_other",
     )(core, *[pltpu.with_memory_space_constraint(x, pltpu.HBM) for x in (grads, errors, q_prev)])
+
+
+def correct_own(g, e, q, c_oth):
+    return pl.pallas_call(
+        own_kernel,
+        in_specs=in_vmem(4),
+        out_specs=in_vmem(2) + in_hbm(1),
+        out_shape=[pltpu.VMEM((ROWS, COLS), F32), pltpu.VMEM((RANK, ROWS), F32), pltpu.HBM((ROWS, COLS), F32)],
+        scratch_shapes=[pltpu.SemaphoreType.DMA],
+        compiler_params=params(),
+        cost_estimate=pl.CostEstimate(flops=150_000_000, bytes_accessed=4_000_000, transcendentals=0),
+        name="correct_own",
+    )(g, e, q, c_oth)
 
 
 def right_kernel(parts, c_own, c_got, raw, left):
@@ -144,6 +173,34 @@
         cost_estimate=pl.CostEstimate(flops=100_000_000, bytes_accessed=4_000_000, transcendentals=0),
         name="right_terms",
     )(parts, c_own, c_got)
+
+
+def spread_kernel(parts, out, buf, sems):
+    total = jnp.sum(parts[...], axis=0)
+    group = RANK // GROUPS
+    for k in range(group):
+        buf[k] = total
+    sends = [pltpu.make_async_copy(buf, out.at[pl.ds(g * group, group)], sems.at[g]) for g in range(GROUPS)]
+    for copy in sends:
+        copy.start()
+    for copy in sends:
+        copy.wait()
+
+
+def spread(parts):
+    return pl.pallas_call(
+        spread_kernel,
+        in_specs=in_vmem(1),
+        out_specs=in_hbm(1)[0],
+        out_shape=pltpu.HBM((RANK, 1, COLS), F32),
+        scratch_shapes=[
+            pltpu.VMEM((RANK // GROUPS, 1, COLS), F32),
+            pltpu.SemaphoreType.DMA((GROUPS,)),
+        ],
+        compiler_params=params(),
+        cost_estimate=pl.CostEstimate(flops=100_000, bytes_accessed=1_000_000, transcendentals=0),
+        name="spread",
+    )(parts)
 
 
 def factor_kernel(left_ref, out):
@@ -248,19 +305,20 @@
 
 def shards(grads, errors, q_prev):
     core = lax.axis_index("core").astype(jnp.int32)
-    c_own, c_oth, left_own, left_oth = correct(core[None], grads, errors, q_prev)
+    c_oth, left_oth, g_own, e_own, q_own = correct_other(core[None], grads, errors, q_prev)
     left_got = swap(left_oth)
+    c_own, left_own, c_oth = correct_own(g_own, e_own, q_own, c_oth)
     left_got, c_oth = lax.optimization_barrier((left_got, c_oth))
     left = left_own + left_got
     c_got = swap(c_oth)
     left = jnp.sum(copies(left, ("x", "tensor")), axis=0)
     parts = copies(left, ("z",))
     raw, left = right(parts, c_own, c_got)
-    mine = jnp.sum(lax.all_to_all(raw, ("z", "x"), 0, 0, tiled=True), axis=0)
+    mine = spread(lax.all_to_all(raw, ("z", "x"), 0, 0, tiled=True))
     mine, left = lax.optimization_barrier((mine, left))
     factors = factor(left)
     factors_got = swap(factors)
-    raw = copies(mine, ("z", "x"))
+    raw = lax.all_to_all(mine, ("z", "x"), 0, 0, tiled=True)
     raw, factors, factors_got = lax.optimization_barrier((raw, factors, factors_got))
     raw_got = swap(raw)
     outs = finish(core[None], raw, factors, c_own)

time: 80.8 us -> 79.5 us (0.984)
  Pallas kernels: 11 us -> 12.8 us
  waiting for transfers between devices: 5.84 us -> 4.74 us
  local copies, waits for them, and re-layouts: 1.01 us -> 0.03 us
    pallas_call x1 -> x3, Pallas kernels: 3.59 us -> 5.39 us  [the longest x1 3.18 us: correct_other(): pl.pallas_call(other_kernel, in_specs=[SCALAR] + in_hbm(3), out_specs=in_...]
    broadcast_in_dim x3 -> x2, local copies, waits for them, and re-layouts: 0.99 us -> 0.03 us  [copies(): jnp.broadcast_to(value[None], (count,) + value.shape)]
    ppermute x4, waiting for transfers between devices: 1.7 us -> 0.87 us  [swap(): return lax.ppermute(value, 'core', [(0, 1), (1, 0)])]
  transfers between devices with their start and end apart: 5 -> 5, of which waited for: 3 -> 2; matrix products, arithmetic and copies ran while one was open for 0% -> 0% of each run, Pallas kernels for 6% -> 8%
where the time goes in v5:
time: 79.5 us; the launch traced here: 79.2 us
  blocking collectives  43.2 us (54%)
  starting transfers between devices  17.6 us (22%)
  Pallas kernels  12.8 us (16%)
  waiting for transfers between devices  4.74 us (6%)
    all_to_all x2, blocking collectives, copies(): lax.all_to_all(jnp.broadcast_to(value[None], (count,) + value.shape), axe...  28.3 us
    all_to_all x1, blocking collectives, shards(): mine = spread(lax.all_to_all(raw, ('z', 'x'), 0, 0, tiled=True))  14.9 us
    ppermute x4, starting transfers between devices, swap(): return lax.ppermute(value, 'core', [(0, 1), (1, 0)])  12.4 us
    all_to_all x1, starting transfers between devices, shards(): raw = lax.all_to_all(mine, ('z', 'x'), 0, 0, tiled=True)  5.27 us
    all_to_all x1, waiting for transfers between devices, shards(): raw = lax.all_to_all(mine, ('z', 'x'), 0, 0, tiled=True)  3.87 us
    pallas_call x2, Pallas kernels, finish(): pl.pallas_call(finish_kernel, in_specs=[SCALAR] + in_vmem(3) + anywhere(l...  3.77 us
    pallas_call x1, Pallas kernels, correct_other(): pl.pallas_call(other_kernel, in_specs=[SCALAR] + in_hbm(3), out_specs=in_...  3.18 us
    pallas_call x1, Pallas kernels, factor(): pl.pallas_call(factor_kernel, in_specs=in_vmem(1), out_specs=in_vmem(1)[0...  3.15 us
  transfers between devices with their start and end apart: 5, of which 2 were waited for; matrix products, arithmetic and copies ran while one was open for 0% of the time, Pallas kernels for 8%

profile of v5, /device:TPU:1, one launch (start us, length us, event | category | flops | bytes accessed | tf_op | source)
XLA Modules:
  0.0 79.2 jit_solution(10960361685564296803)
XLA Ops:
  0.6 3.2 %correct_other.1 = (f32[128,3200]{1,0:T(8,128)S(1)}, f32[32,128]{1,0:T(8,128)S(1)}, bf16[128,3200]{1,0:T(8,128)(2,1)S(1)}, f32[128,3200]{1,0:T(8,128)S(1)}, f32[32,3200]{1,0:T(8,128)S(1)}) custom-call(s32[1]{0:T(128)} %bitcast.core_ref.which_ref, bf16[2,1,128,3200]{3,2,1,0:T(8,128)(2,1)} %grads.1, f32[2,1,128,3200]{3,2,1,0:T(8,128)} %errors.1, ...), custom_call_target="tpu_custom_call" | custom-call | flops 150000000 | bytes 9000000 | tf_op jit(solution)/shard_map/correct_other/pallas_call | solution.py:113
  3.8 3.3 %collective-permute-start = (f32[32,128]{1,0:T(8,128)S(1)}, f32[32,128]{1,0:T(8,128)S(1)}, u32[]{:S(2)}, u32[]{:S(2)}) collective-permute-start(f32[32,128]{1,0:T(8,128)S(1)} %get-tuple-element.28), channel_id=1, source_target_pairs={{0,4},{4,0},{1,5},{5,1},{2,6},{6,2},{3,7},{7,3},{8,12},{12,8},{9,1... | collective-permute-start | bytes 49160 | tf_op jit(solution)/shard_map/ppermute | solution.py:296
  7.2 1.2 %correct_own.1 = (f32[128,3200]{1,0:T(8,128)S(1)}, f32[32,128]{1,0:T(8,128)S(1)}, f32[128,3200]{1,0:T(8,128)}) custom-call(bf16[128,3200]{1,0:T(8,128)(2,1)S(1)} %get-tuple-element.23.g, f32[128,3200]{1,0:T(8,128)S(1)} %get-tuple-element.24.e, f32[32,3200]{1,0:T(8,128)S(1)} %get-tuple-element.25.q, f32[128,3200]{1,0:T(8,128)S(1)} %get-tuple-element.26.c_oth), custom_call_target="tpu_custom_call" | custom-call | flops 150000000 | bytes 4000000 | tf_op jit(solution)/shard_map/correct_own/pallas_call | solution.py:137
  8.4 0.0 collective-permute-done
  8.4 0.1 collective-permute-start.1
  8.5 12.3 %all_to_all.20 = f32[16,32,128]{2,1,0:T(8,128)S(1)} all-to-all(f32[16,32,128]{2,1,0:T(8,128)S(1)} %broadcast_in_dim.7), channel_id=1, replica_groups=mesh['z'=8,'x'=4,'core'=2,'tensor'=4] {'x','tensor'}, dimensions={0} | all-to-all | bytes 524288 | tf_op jit(solution)/shard_map/all_to_all | solution.py:303
  20.8 16.0 %all_to_all.21.parts = f32[8,32,128]{2,1,0:T(8,128)S(1)} all-to-all(f32[8,32,128]{2,1,0:T(8,128)S(1)} %broadcast_in_dim.8), channel_id=1, replica_groups=mesh['z'=8,'x'=4,'core'=2,'tensor'=4] {'z'}, dimensions={0} | all-to-all | bytes 262144 | tf_op jit(solution)/shard_map/all_to_all | solution.py:303
  36.9 0.0 collective-permute-done.1.c_got
  36.9 0.5 right_terms.1
  37.3 14.9 %all_to_all.22.parts = f32[32,1,3200]{2,1,0:T(1,128)S(1)} all-to-all(f32[32,1,3200]{2,1,0:T(1,128)S(1)} %get-tuple-element.33), channel_id=1, replica_groups=mesh['z'=8,'x'=4,'core'=2,'tensor'=4] {'z','x'}, dimensions={0} | all-to-all | bytes 819200 | tf_op jit(solution)/shard_map/all_to_all | solution.py:317
  52.2 1.0 %spread.1 = f32[32,1,3200]{2,1,0:T(1,128)} custom-call(f32[32,1,3200]{2,1,0:T(1,128)S(1)} %all_to_all.22.parts), custom_call_target="tpu_custom_call" | custom-call | flops 100000 | bytes 1000000 | tf_op jit(solution)/shard_map/spread/pallas_call | solution.py:191
  53.3 5.3 %all-to-all-start.3 = ((f32[32,1,3200]{2,1,0:T(1,128)}), f32[32,1,3200]{2,1,0:T(1,128)S(1)}, u32[]{:S(2)}, u32[]{:S(2)}) async-start(f32[32,1,3200]{2,1,0:T(1,128)} %spread.1), calls=%async_computation.3 | async-start | bytes 819200 | tf_op jit(solution)/shard_map/all_to_all | solution.py:321
  58.6 3.1 %factor.1.factors = f32[2,32,128]{2,1,0:T(8,128)S(1)} custom-call(f32[32,128]{1,0:T(8,128)S(1)} %get-tuple-element.36.left_ref), custom_call_target="tpu_custom_call" | custom-call | flops 10000000 | bytes 10000000 | tf_op jit(solution)/shard_map/factor/pallas_call | solution.py:236
  61.7 3.7 %collective-permute-start.2 = (f32[2,32,128]{2,1,0:T(8,128)S(1)}, f32[2,32,128]{2,1,0:T(8,128)S(1)}, u32[]{:S(2)}, u32[]{:S(2)}) collective-permute-start(f32[2,32,128]{2,1,0:T(8,128)S(1)} %factor.1.factors), channel_id=1, source_target_pairs={{0,4},{4,0},{1,5},{5,1},{2,6},{6,2},{3,7},{7,3},{8,12},{12,8},{9,1... | collective-permute-start | bytes 98312 | tf_op jit(solution)/shard_map/ppermute | solution.py:296
  65.4 0.9 %collective-permute-done.2.factors = f32[2,32,128]{2,1,0:T(8,128)S(1)} collective-permute-done((f32[2,32,128]{2,1,0:T(8,128)S(1)}, f32[2,32,128]{2,1,0:T(8,128)S(1)}, u32[]{:S(2)}, u32[]{:S(2)}) %collective-permute-start.2) | collective-permute-done | bytes 32800 | tf_op jit(solution)/shard_map/ppermute | solution.py:296
  66.3 3.9 %all-to-all-done.3.raw = f32[32,1,3200]{2,1,0:T(1,128)S(1)} async-done(((f32[32,1,3200]{2,1,0:T(1,128)}), f32[32,1,3200]{2,1,0:T(1,128)S(1)}, u32[]{:S(2)}, u32[]{:S(2)}) %all-to-all-start.3) | async-done | bytes 409632 | tf_op jit(solution)/shard_map/all_to_all | solution.py:321
  70.2 0.0 copy-start
  70.2 5.2 %collective-permute-start.3 = (f32[32,1,3200]{2,1,0:T(1,128)S(1)}, f32[32,1,3200]{2,1,0:T(1,128)S(1)}, u32[]{:S(2)}, u32[]{:S(2)}) collective-permute-start(f32[32,1,3200]{2,1,0:T(1,128)S(1)} %all-to-all-done.3.raw), channel_id=1, source_target_pairs={{0,4},{4,0},{1,5},{5,1},{2,6},{6,2},{3,7},{7,3},{8,12},{12,8},{9,1... | collective-permute-start | bytes 1228808 | tf_op jit(solution)/shard_map/ppermute | solution.py:296
  75.4 1.9 %finish_first.1 = (bf16[2,128,3200]{2,1,0:T(8,128)(2,1)}, f32[2,1,128,3200]{3,2,1,0:T(8,128)}, f32[2,32,3200]{2,1,0:T(8,128)}) custom-call(s32[1]{0:T(128)} %bitcast.core_ref.which_ref, f32[32,1,3200]{2,1,0:T(1,128)S(1)} %all-to-all-done.3.raw, f32[2,32,128]{2,1,0:T(8,128)S(1)} %factor.1.factors, f32[128,3200]{1,0:T(8,128)S(1)} %get-tuple-element.31.c_own.c), custom_call_target="tpu_custom_call" | custom-call | flops 50000000 | bytes 6000000 | tf_op jit(solution)/shard_map/finish_first/pallas_call | solution.py:273
  77.2 0.0 collective-permute-done.3.raw
  77.3 0.0 copy-done
  77.3 1.9 %finish_second.1 = (bf16[2,128,3200]{2,1,0:T(8,128)(2,1)}, f32[2,1,128,3200]{3,2,1,0:T(8,128)}, f32[2,32,3200]{2,1,0:T(8,128)}) custom-call(s32[1]{0:T(128)S(6)} %sub.3.which_ref, f32[32,1,3200]{2,1,0:T(1,128)S(1)} %collective-permute-done.3.raw, ...), custom_call_target="tpu_custom_call", output_to_operand_aliasing={{0}: (4, {}), {1}: (5, {}), {2}: (6, {})} | custom-call | flops 50000000 | bytes 6000000 | tf_op jit(solution)/shard_map/finish_second/pallas_call | solution.py:273
  (4 shorter events, 0.1 us)
Async XLA Ops:
  3.8 4.5 %collective-permute-start = (f32[32,128]{1,0:T(8,128)S(1)}, f32[32,128]{1,0:T(8,128)S(1)}, u32[]{:S(2)}, u32[]{:S(2)}) collective-permute-start(f32[32,128]{1,0:T(8,128)S(1)} %get-tuple-element.28), channel_id=1, source_target_pairs={{0,4},{4,0},{1,5},{5,1},{2,6},{6,2},{3,7},{7,3},{8,12},{12,8},{9,1... | collective-permute-start | bytes 49160 | tf_op jit(solution)/shard_map/ppermute | solution.py:296
  8.4 28.5 %collective-permute-start.1 = (f32[128,3200]{1,0:T(8,128)}, f32[128,3200]{1,0:T(8,128)S(1)}, u32[]{:S(2)}, u32[]{:S(2)}) collective-permute-start(f32[128,3200]{1,0:T(8,128)} %get-tuple-element.32.c), channel_id=1, source_target_pairs={{0,4},{4,0},{1,5},{5,1},{2,6},{6,2},{3,7},{7,3},{8,12},{12,8},{9,1... | collective-permute-start | bytes 4915208 | tf_op jit(solution)/shard_map/ppermute | solution.py:296
  53.3 16.9 %all-to-all-start.3 = ((f32[32,1,3200]{2,1,0:T(1,128)}), f32[32,1,3200]{2,1,0:T(1,128)S(1)}, u32[]{:S(2)}, u32[]{:S(2)}) async-start(f32[32,1,3200]{2,1,0:T(1,128)} %spread.1), calls=%async_computation.3 | async-start | bytes 819200 | tf_op jit(solution)/shard_map/all_to_all | solution.py:321
  61.7 4.6 %collective-permute-start.2 = (f32[2,32,128]{2,1,0:T(8,128)S(1)}, f32[2,32,128]{2,1,0:T(8,128)S(1)}, u32[]{:S(2)}, u32[]{:S(2)}) collective-permute-start(f32[2,32,128]{2,1,0:T(8,128)S(1)} %factor.1.factors), channel_id=1, source_target_pairs={{0,4},{4,0},{1,5},{5,1},{2,6},{6,2},{3,7},{7,3},{8,12},{12,8},{9,1... | collective-permute-start | bytes 98312 | tf_op jit(solution)/shard_map/ppermute | solution.py:296
  70.2 7.1 %copy-start = (f32[128,3200]{1,0:T(8,128)S(1)}, f32[128,3200]{1,0:T(8,128)}, u32[]{:S(2)}) copy-start(f32[128,3200]{1,0:T(8,128)} %get-tuple-element.32.c) | copy-start | bytes 4915204
  70.2 7.1 %collective-permute-start.3 = (f32[32,1,3200]{2,1,0:T(1,128)S(1)}, f32[32,1,3200]{2,1,0:T(1,128)S(1)}, u32[]{:S(2)}, u32[]{:S(2)}) collective-permute-start(f32[32,1,3200]{2,1,0:T(1,128)S(1)} %all-to-all-done.3.raw), channel_id=1, source_target_pairs={{0,4},{4,0},{1,5},{5,1},{2,6},{6,2},{3,7},{7,3},{8,12},{12,8},{9,1... | collective-permute-start | bytes 1228808 | tf_op jit(solution)/shard_map/ppermute | solution.py:296

commit v6 on v5

--- a/solution.py
+++ b/solution.py
@@ -34,8 +34,9 @@
 def left_terms(c, q):
     c_hi, c_lo = split(c)
     q_hi, q_lo = split(q)
-    both = matmul(jnp.concatenate([q_hi, q_lo], axis=0), c_hi, ((1,), (1,)))
-    return both[:RANK] + both[RANK:] + matmul(q_hi, c_lo, ((1,), (1,)))
+    q_both = jnp.concatenate([q_hi, q_lo], axis=0)
+    both = matmul(q_both, c_hi, ((1,), (1,))) + matmul(q_both, c_lo, ((1,), (1,)))
+    return both[:RANK] + both[RANK:]
 
 
 def other_kernel(
@@ -151,11 +152,12 @@
     left[...] = total
     l_hi, l_lo = split(total)
     l_both = jnp.concatenate([l_hi, l_lo], axis=0)
+    l_both = jnp.concatenate([l_both, l_both], axis=1)
     for first, width in PIECES:
         cols = pl.ds(first, width)
         s_hi, s_lo = split(c_own[:, cols] + c_got[:, cols])
-        both = matmul(l_both, s_hi, ((1,), (0,)))
-        value = both[:RANK] + both[RANK:] + matmul(l_hi, s_lo, ((1,), (0,)))
+        both = matmul(l_both, jnp.concatenate([s_hi, s_lo], axis=0), ((1,), (0,)))
+        value = both[:RANK] + both[RANK:]
         for k in range(RANK):
             raw[k, :, cols] = value[k : k + 1]
 
@@ -248,13 +250,13 @@
     rebuilt, new_errors, new_q, r_buf, e_buf, q_buf, sems = refs[-7:]
     m = which_ref[0]
     f_hi, f_lo = split(jnp.concatenate([factors[0], factors[1][:, :RANK]], axis=1))
-    f_all = jnp.concatenate([f_hi, f_hi, f_lo], axis=0)
+    f_all = jnp.concatenate([f_hi, f_hi, f_lo, f_lo], axis=0)
     out = []
     for j, (first, width) in enumerate(OUT_PIECES):
         cols = pl.ds(first, width)
         rows = jnp.concatenate([raw[k, :, cols] for k in range(RANK)], axis=0)
         r_hi, r_lo = split(rows)
-        both = matmul(f_all, jnp.concatenate([r_hi, r_lo, r_hi], axis=0), ((0,), (0,)))
+        both = matmul(f_all, jnp.concatenate([r_hi, r_lo, r_hi, r_lo], axis=0), ((0,), (0,)))
         approx = both[:ROWS]
         e_buf[:, cols] = c[:, cols] - approx
         out.append(pltpu.make_async_copy(e_buf.at[:, cols], new_errors.at[m, 0, :, cols], sems.at[3 * j]))

time: 79.5 us -> 79.5 us (level)
  no operation moved by 1% of the time
where the time goes in v6:
time: 79.5 us; the launch traced here: 79.2 us
  blocking collectives  43.2 us (54%)
  starting transfers between devices  17.6 us (22%)
  Pallas kernels  12.9 us (16%)
  waiting for transfers between devices  4.73 us (6%)
    all_to_all x2, blocking collectives, copies(): lax.all_to_all(jnp.broadcast_to(value[None], (count,) + value.shape), axe...  28.3 us
    all_to_all x1, blocking collectives, shards(): mine = spread(lax.all_to_all(raw, ('z', 'x'), 0, 0, tiled=True))  14.9 us
    ppermute x4, starting transfers between devices, swap(): return lax.ppermute(value, 'core', [(0, 1), (1, 0)])  12.4 us
    all_to_all x1, starting transfers between devices, shards(): raw = lax.all_to_all(mine, ('z', 'x'), 0, 0, tiled=True)  5.27 us
    all_to_all x1, waiting for transfers between devices, shards(): raw = lax.all_to_all(mine, ('z', 'x'), 0, 0, tiled=True)  3.87 us
    pallas_call x2, Pallas kernels, finish(): pl.pallas_call(finish_kernel, in_specs=[SCALAR] + in_vmem(3) + anywhere(l...  3.81 us
    pallas_call x1, Pallas kernels, correct_other(): pl.pallas_call(other_kernel, in_specs=[SCALAR] + in_hbm(3), out_specs=in_...  3.21 us
    pallas_call x1, Pallas kernels, factor(): pl.pallas_call(factor_kernel, in_specs=in_vmem(1), out_specs=in_vmem(1)[0...  3.15 us
  transfers between devices with their start and end apart: 5, of which 2 were waited for; matrix products, arithmetic and copies ran while one was open for 0% of the time, Pallas kernels for 8%

profile of v6, /device:TPU:1, one launch (start us, length us, event | category | flops | bytes accessed | tf_op | source)
XLA Modules:
  0.0 79.2 jit_solution(2711027872081761603)
XLA Ops:
  0.6 3.2 %correct_other.1 = (f32[128,3200]{1,0:T(8,128)S(1)}, f32[32,128]{1,0:T(8,128)S(1)}, bf16[128,3200]{1,0:T(8,128)(2,1)S(1)}, f32[128,3200]{1,0:T(8,128)S(1)}, f32[32,3200]{1,0:T(8,128)S(1)}) custom-call(s32[1]{0:T(128)} %bitcast.core_ref.which_ref, bf16[2,1,128,3200]{3,2,1,0:T(8,128)(2,1)} %grads.1, f32[2,1,128,3200]{3,2,1,0:T(8,128)} %errors.1, ...), custom_call_target="tpu_custom_call" | custom-call | flops 150000000 | bytes 9000000 | tf_op jit(solution)/shard_map/correct_other/pallas_call | solution.py:114
  3.8 3.3 %collective-permute-start = (f32[32,128]{1,0:T(8,128)S(1)}, f32[32,128]{1,0:T(8,128)S(1)}, u32[]{:S(2)}, u32[]{:S(2)}) collective-permute-start(f32[32,128]{1,0:T(8,128)S(1)} %get-tuple-element.28), channel_id=1, source_target_pairs={{0,4},{4,0},{1,5},{5,1},{2,6},{6,2},{3,7},{7,3},{8,12},{12,8},{9,1... | collective-permute-start | bytes 49160 | tf_op jit(solution)/shard_map/ppermute | solution.py:298
  7.2 1.2 %correct_own.1 = (f32[128,3200]{1,0:T(8,128)S(1)}, f32[32,128]{1,0:T(8,128)S(1)}, f32[128,3200]{1,0:T(8,128)}) custom-call(bf16[128,3200]{1,0:T(8,128)(2,1)S(1)} %get-tuple-element.23.g, f32[128,3200]{1,0:T(8,128)S(1)} %get-tuple-element.24.e, f32[32,3200]{1,0:T(8,128)S(1)} %get-tuple-element.25.q, f32[128,3200]{1,0:T(8,128)S(1)} %get-tuple-element.26.c_oth), custom_call_target="tpu_custom_call" | custom-call | flops 150000000 | bytes 4000000 | tf_op jit(solution)/shard_map/correct_own/pallas_call | solution.py:138
  8.4 0.0 collective-permute-done
  8.4 0.1 collective-permute-start.1
  8.5 12.3 %all_to_all.20 = f32[16,32,128]{2,1,0:T(8,128)S(1)} all-to-all(f32[16,32,128]{2,1,0:T(8,128)S(1)} %broadcast_in_dim.7), channel_id=1, replica_groups=mesh['z'=8,'x'=4,'core'=2,'tensor'=4] {'x','tensor'}, dimensions={0} | all-to-all | bytes 524288 | tf_op jit(solution)/shard_map/all_to_all | solution.py:305
  20.9 16.0 %all_to_all.21.parts = f32[8,32,128]{2,1,0:T(8,128)S(1)} all-to-all(f32[8,32,128]{2,1,0:T(8,128)S(1)} %broadcast_in_dim.8), channel_id=1, replica_groups=mesh['z'=8,'x'=4,'core'=2,'tensor'=4] {'z'}, dimensions={0} | all-to-all | bytes 262144 | tf_op jit(solution)/shard_map/all_to_all | solution.py:305
  36.9 0.0 collective-permute-done.1.c_got
  36.9 0.5 right_terms.1
  37.4 14.9 %all_to_all.22.parts = f32[32,1,3200]{2,1,0:T(1,128)S(1)} all-to-all(f32[32,1,3200]{2,1,0:T(1,128)S(1)} %get-tuple-element.33), channel_id=1, replica_groups=mesh['z'=8,'x'=4,'core'=2,'tensor'=4] {'z','x'}, dimensions={0} | all-to-all | bytes 819200 | tf_op jit(solution)/shard_map/all_to_all | solution.py:319
  52.3 1.0 %spread.1 = f32[32,1,3200]{2,1,0:T(1,128)} custom-call(f32[32,1,3200]{2,1,0:T(1,128)S(1)} %all_to_all.22.parts), custom_call_target="tpu_custom_call" | custom-call | flops 100000 | bytes 1000000 | tf_op jit(solution)/shard_map/spread/pallas_call | solution.py:193
  53.3 5.3 %all-to-all-start.3 = ((f32[32,1,3200]{2,1,0:T(1,128)}), f32[32,1,3200]{2,1,0:T(1,128)S(1)}, u32[]{:S(2)}, u32[]{:S(2)}) async-start(f32[32,1,3200]{2,1,0:T(1,128)} %spread.1), calls=%async_computation.3 | async-start | bytes 819200 | tf_op jit(solution)/shard_map/all_to_all | solution.py:323
  58.6 3.1 %factor.1.factors = f32[2,32,128]{2,1,0:T(8,128)S(1)} custom-call(f32[32,128]{1,0:T(8,128)S(1)} %get-tuple-element.36.left_ref), custom_call_target="tpu_custom_call" | custom-call | flops 10000000 | bytes 10000000 | tf_op jit(solution)/shard_map/factor/pallas_call | solution.py:238
  61.7 3.7 %collective-permute-start.2 = (f32[2,32,128]{2,1,0:T(8,128)S(1)}, f32[2,32,128]{2,1,0:T(8,128)S(1)}, u32[]{:S(2)}, u32[]{:S(2)}) collective-permute-start(f32[2,32,128]{2,1,0:T(8,128)S(1)} %factor.1.factors), channel_id=1, source_target_pairs={{0,4},{4,0},{1,5},{5,1},{2,6},{6,2},{3,7},{7,3},{8,12},{12,8},{9,1... | collective-permute-start | bytes 98312 | tf_op jit(solution)/shard_map/ppermute | solution.py:298
  65.5 0.9 %collective-permute-done.2.factors = f32[2,32,128]{2,1,0:T(8,128)S(1)} collective-permute-done((f32[2,32,128]{2,1,0:T(8,128)S(1)}, f32[2,32,128]{2,1,0:T(8,128)S(1)}, u32[]{:S(2)}, u32[]{:S(2)}) %collective-permute-start.2) | collective-permute-done | bytes 32800 | tf_op jit(solution)/shard_map/ppermute | solution.py:298
  66.3 3.9 %all-to-all-done.3.raw = f32[32,1,3200]{2,1,0:T(1,128)S(1)} async-done(((f32[32,1,3200]{2,1,0:T(1,128)}), f32[32,1,3200]{2,1,0:T(1,128)S(1)}, u32[]{:S(2)}, u32[]{:S(2)}) %all-to-all-start.3) | async-done | bytes 409632 | tf_op jit(solution)/shard_map/all_to_all | solution.py:323
  70.2 0.0 copy-start
  70.2 5.2 %collective-permute-start.3 = (f32[32,1,3200]{2,1,0:T(1,128)S(1)}, f32[32,1,3200]{2,1,0:T(1,128)S(1)}, u32[]{:S(2)}, u32[]{:S(2)}) collective-permute-start(f32[32,1,3200]{2,1,0:T(1,128)S(1)} %all-to-all-done.3.raw), channel_id=1, source_target_pairs={{0,4},{4,0},{1,5},{5,1},{2,6},{6,2},{3,7},{7,3},{8,12},{12,8},{9,1... | collective-permute-start | bytes 1228808 | tf_op jit(solution)/shard_map/ppermute | solution.py:298
  75.4 1.9 %finish_first.1 = (bf16[2,128,3200]{2,1,0:T(8,128)(2,1)}, f32[2,1,128,3200]{3,2,1,0:T(8,128)}, f32[2,32,3200]{2,1,0:T(8,128)}) custom-call(s32[1]{0:T(128)} %bitcast.core_ref.which_ref, f32[32,1,3200]{2,1,0:T(1,128)S(1)} %all-to-all-done.3.raw, f32[2,32,128]{2,1,0:T(8,128)S(1)} %factor.1.factors, f32[128,3200]{1,0:T(8,128)S(1)} %get-tuple-element.31.c_own.c), custom_call_target="tpu_custom_call" | custom-call | flops 50000000 | bytes 6000000 | tf_op jit(solution)/shard_map/finish_first/pallas_call | solution.py:275
  77.3 0.0 collective-permute-done.3.raw
  77.3 0.0 copy-done
  77.3 1.9 %finish_second.1 = (bf16[2,128,3200]{2,1,0:T(8,128)(2,1)}, f32[2,1,128,3200]{3,2,1,0:T(8,128)}, f32[2,32,3200]{2,1,0:T(8,128)}) custom-call(s32[1]{0:T(128)S(6)} %sub.3.which_ref, f32[32,1,3200]{2,1,0:T(1,128)S(1)} %collective-permute-done.3.raw, ...), custom_call_target="tpu_custom_call", output_to_operand_aliasing={{0}: (4, {}), {1}: (5, {}), {2}: (6, {})} | custom-call | flops 50000000 | bytes 6000000 | tf_op jit(solution)/shard_map/finish_second/pallas_call | solution.py:275
  (4 shorter events, 0.1 us)
Async XLA Ops:
  3.8 4.5 %collective-permute-start = (f32[32,128]{1,0:T(8,128)S(1)}, f32[32,128]{1,0:T(8,128)S(1)}, u32[]{:S(2)}, u32[]{:S(2)}) collective-permute-start(f32[32,128]{1,0:T(8,128)S(1)} %get-tuple-element.28), channel_id=1, source_target_pairs={{0,4},{4,0},{1,5},{5,1},{2,6},{6,2},{3,7},{7,3},{8,12},{12,8},{9,1... | collective-permute-start | bytes 49160 | tf_op jit(solution)/shard_map/ppermute | solution.py:298
  8.4 28.5 %collective-permute-start.1 = (f32[128,3200]{1,0:T(8,128)}, f32[128,3200]{1,0:T(8,128)S(1)}, u32[]{:S(2)}, u32[]{:S(2)}) collective-permute-start(f32[128,3200]{1,0:T(8,128)} %get-tuple-element.32.c), channel_id=1, source_target_pairs={{0,4},{4,0},{1,5},{5,1},{2,6},{6,2},{3,7},{7,3},{8,12},{12,8},{9,1... | collective-permute-start | bytes 4915208 | tf_op jit(solution)/shard_map/ppermute | solution.py:298
  53.3 16.9 %all-to-all-start.3 = ((f32[32,1,3200]{2,1,0:T(1,128)}), f32[32,1,3200]{2,1,0:T(1,128)S(1)}, u32[]{:S(2)}, u32[]{:S(2)}) async-start(f32[32,1,3200]{2,1,0:T(1,128)} %spread.1), calls=%async_computation.3 | async-start | bytes 819200 | tf_op jit(solution)/shard_map/all_to_all | solution.py:323
  61.7 4.6 %collective-permute-start.2 = (f32[2,32,128]{2,1,0:T(8,128)S(1)}, f32[2,32,128]{2,1,0:T(8,128)S(1)}, u32[]{:S(2)}, u32[]{:S(2)}) collective-permute-start(f32[2,32,128]{2,1,0:T(8,128)S(1)} %factor.1.factors), channel_id=1, source_target_pairs={{0,4},{4,0},{1,5},{5,1},{2,6},{6,2},{3,7},{7,3},{8,12},{12,8},{9,1... | collective-permute-start | bytes 98312 | tf_op jit(solution)/shard_map/ppermute | solution.py:298
  70.2 7.1 %copy-start = (f32[128,3200]{1,0:T(8,128)S(1)}, f32[128,3200]{1,0:T(8,128)}, u32[]{:S(2)}) copy-start(f32[128,3200]{1,0:T(8,128)} %get-tuple-element.32.c) | copy-start | bytes 4915204
  70.2 7.1 %collective-permute-start.3 = (f32[32,1,3200]{2,1,0:T(1,128)S(1)}, f32[32,1,3200]{2,1,0:T(1,128)S(1)}, u32[]{:S(2)}, u32[]{:S(2)}) collective-permute-start(f32[32,1,3200]{2,1,0:T(1,128)S(1)} %all-to-all-done.3.raw), channel_id=1, source_target_pairs={{0,4},{4,0},{1,5},{5,1},{2,6},{6,2},{3,7},{7,3},{8,12},{12,8},{9,1... | collective-permute-start | bytes 1228808 | tf_op jit(solution)/shard_map/ppermute | solution.py:298

commit v7 on v6

--- a/solution.py
+++ b/solution.py
@@ -13,6 +13,7 @@
 ROWS = 128
 COLS = 3200
 PIECES = ((0, 1280), (1280, 1920))
+IN_PIECES = ((0, 1024), (1024, 1024), (2048, 768), (2816, 384))
 GROUPS = 4
 OUT_PIECES = ((0, 640), (640, 1280), (1920, 1280))
 VMEM_BYTES = 24 * 1024 * 1024
@@ -44,9 +45,9 @@
 ):
     own = core_ref[0]
     oth = 1 - own
-    count = len(PIECES)
+    count = len(IN_PIECES)
     arrivals = []
-    for j, (first, width) in enumerate(PIECES):
+    for j, (first, width) in enumerate(IN_PIECES):
         cols = pl.ds(first, width)
         arrivals.append(
             (
@@ -68,7 +69,7 @@
     for copy in keeps:
         copy.start()
     total = jnp.zeros((RANK, ROWS), F32)
-    for j, (first, width) in enumerate(PIECES):
+    for j, (first, width) in enumerate(IN_PIECES):
         cols = pl.ds(first, width)
         for copy in arrivals[j]:
             copy.wait()
@@ -125,7 +126,7 @@
         scratch_shapes=[
             pltpu.VMEM((ROWS, COLS), BF16),
             pltpu.VMEM((RANK, COLS), F32),
-            pltpu.SemaphoreType.DMA((2 * len(PIECES) + 1,)),
+            pltpu.SemaphoreType.DMA((2 * len(IN_PIECES) + 1,)),
             pltpu.SemaphoreType.DMA((3,)),
         ],
         compiler_params=params(),

time: 79.5 us -> 79.2 us (level)
  no operation moved by 1% of the time
where the time goes in v7:
time: 79.2 us; the launch traced here: 78.9 us
  blocking collectives  43.2 us (55%)
  starting transfers between devices  17.6 us (22%)
  Pallas kernels  12.5 us (16%)
  waiting for transfers between devices  4.73 us (6%)
    all_to_all x2, blocking collectives, copies(): lax.all_to_all(jnp.broadcast_to(value[None], (count,) + value.shape), axe...  28.3 us
    all_to_all x1, blocking collectives, shards(): mine = spread(lax.all_to_all(raw, ('z', 'x'), 0, 0, tiled=True))  14.9 us
    ppermute x4, starting transfers between devices, swap(): return lax.ppermute(value, 'core', [(0, 1), (1, 0)])  12.4 us
    all_to_all x1, starting transfers between devices, shards(): raw = lax.all_to_all(mine, ('z', 'x'), 0, 0, tiled=True)  5.27 us
    all_to_all x1, waiting for transfers between devices, shards(): raw = lax.all_to_all(mine, ('z', 'x'), 0, 0, tiled=True)  3.87 us
    pallas_call x2, Pallas kernels, finish(): pl.pallas_call(finish_kernel, in_specs=[SCALAR] + in_vmem(3) + anywhere(l...  3.8 us
    pallas_call x1, Pallas kernels, factor(): pl.pallas_call(factor_kernel, in_specs=in_vmem(1), out_specs=in_vmem(1)[0...  3.15 us
    pallas_call x1, Pallas kernels, correct_other(): pl.pallas_call(other_kernel, in_specs=[SCALAR] + in_hbm(3), out_specs=in_...  2.86 us
  transfers between devices with their start and end apart: 5, of which 2 were waited for; matrix products, arithmetic and copies ran while one was open for 0% of the time, Pallas kernels for 8%

profile of v7, /device:TPU:1, one launch (start us, length us, event | category | flops | bytes accessed | tf_op | source)
XLA Modules:
  0.0 78.9 jit_solution(17707127223772967053)
XLA Ops:
  0.6 2.9 %correct_other.1 = (f32[128,3200]{1,0:T(8,128)S(1)}, f32[32,128]{1,0:T(8,128)S(1)}, bf16[128,3200]{1,0:T(8,128)(2,1)S(1)}, f32[128,3200]{1,0:T(8,128)S(1)}, f32[32,3200]{1,0:T(8,128)S(1)}) custom-call(s32[1]{0:T(128)} %bitcast.core_ref.which_ref, bf16[2,1,128,3200]{3,2,1,0:T(8,128)(2,1)} %grads.1, f32[2,1,128,3200]{3,2,1,0:T(8,128)} %errors.1, ...), custom_call_target="tpu_custom_call" | custom-call | flops 150000000 | bytes 9000000 | tf_op jit(solution)/shard_map/correct_other/pallas_call | solution.py:115
  3.5 3.3 %collective-permute-start = (f32[32,128]{1,0:T(8,128)S(1)}, f32[32,128]{1,0:T(8,128)S(1)}, u32[]{:S(2)}, u32[]{:S(2)}) collective-permute-start(f32[32,128]{1,0:T(8,128)S(1)} %get-tuple-element.28), channel_id=1, source_target_pairs={{0,4},{4,0},{1,5},{5,1},{2,6},{6,2},{3,7},{7,3},{8,12},{12,8},{9,1... | collective-permute-start | bytes 49160 | tf_op jit(solution)/shard_map/ppermute | solution.py:299
  6.8 1.2 %correct_own.1 = (f32[128,3200]{1,0:T(8,128)S(1)}, f32[32,128]{1,0:T(8,128)S(1)}, f32[128,3200]{1,0:T(8,128)}) custom-call(bf16[128,3200]{1,0:T(8,128)(2,1)S(1)} %get-tuple-element.23.g, f32[128,3200]{1,0:T(8,128)S(1)} %get-tuple-element.24.e, f32[32,3200]{1,0:T(8,128)S(1)} %get-tuple-element.25.q, f32[128,3200]{1,0:T(8,128)S(1)} %get-tuple-element.26.c_oth), custom_call_target="tpu_custom_call" | custom-call | flops 150000000 | bytes 4000000 | tf_op jit(solution)/shard_map/correct_own/pallas_call | solution.py:139
  8.0 0.0 collective-permute-done
  8.0 0.1 collective-permute-start.1
  8.2 12.3 %all_to_all.20 = f32[16,32,128]{2,1,0:T(8,128)S(1)} all-to-all(f32[16,32,128]{2,1,0:T(8,128)S(1)} %broadcast_in_dim.7), channel_id=1, replica_groups=mesh['z'=8,'x'=4,'core'=2,'tensor'=4] {'x','tensor'}, dimensions={0} | all-to-all | bytes 524288 | tf_op jit(solution)/shard_map/all_to_all | solution.py:306
  20.5 16.0 %all_to_all.21.parts = f32[8,32,128]{2,1,0:T(8,128)S(1)} all-to-all(f32[8,32,128]{2,1,0:T(8,128)S(1)} %broadcast_in_dim.8), channel_id=1, replica_groups=mesh['z'=8,'x'=4,'core'=2,'tensor'=4] {'z'}, dimensions={0} | all-to-all | bytes 262144 | tf_op jit(solution)/shard_map/all_to_all | solution.py:306
  36.5 0.0 collective-permute-done.1.c_got
  36.5 0.5 right_terms.1
  37.0 14.9 %all_to_all.22.parts = f32[32,1,3200]{2,1,0:T(1,128)S(1)} all-to-all(f32[32,1,3200]{2,1,0:T(1,128)S(1)} %get-tuple-element.33), channel_id=1, replica_groups=mesh['z'=8,'x'=4,'core'=2,'tensor'=4] {'z','x'}, dimensions={0} | all-to-all | bytes 819200 | tf_op jit(solution)/shard_map/all_to_all | solution.py:320
  51.9 1.0 %spread.1 = f32[32,1,3200]{2,1,0:T(1,128)} custom-call(f32[32,1,3200]{2,1,0:T(1,128)S(1)} %all_to_all.22.parts), custom_call_target="tpu_custom_call" | custom-call | flops 100000 | bytes 1000000 | tf_op jit(solution)/shard_map/spread/pallas_call | solution.py:194
  52.9 5.3 %all-to-all-start.3 = ((f32[32,1,3200]{2,1,0:T(1,128)}), f32[32,1,3200]{2,1,0:T(1,128)S(1)}, u32[]{:S(2)}, u32[]{:S(2)}) async-start(f32[32,1,3200]{2,1,0:T(1,128)} %spread.1), calls=%async_computation.3 | async-start | bytes 819200 | tf_op jit(solution)/shard_map/all_to_all | solution.py:324
  58.2 3.1 %factor.1.factors = f32[2,32,128]{2,1,0:T(8,128)S(1)} custom-call(f32[32,128]{1,0:T(8,128)S(1)} %get-tuple-element.36.left_ref), custom_call_target="tpu_custom_call" | custom-call | flops 10000000 | bytes 10000000 | tf_op jit(solution)/shard_map/factor/pallas_call | solution.py:239
  61.4 3.7 %collective-permute-start.2 = (f32[2,32,128]{2,1,0:T(8,128)S(1)}, f32[2,32,128]{2,1,0:T(8,128)S(1)}, u32[]{:S(2)}, u32[]{:S(2)}) collective-permute-start(f32[2,32,128]{2,1,0:T(8,128)S(1)} %factor.1.factors), channel_id=1, source_target_pairs={{0,4},{4,0},{1,5},{5,1},{2,6},{6,2},{3,7},{7,3},{8,12},{12,8},{9,1... | collective-permute-start | bytes 98312 | tf_op jit(solution)/shard_map/ppermute | solution.py:299
  65.1 0.9 %collective-permute-done.2.factors = f32[2,32,128]{2,1,0:T(8,128)S(1)} collective-permute-done((f32[2,32,128]{2,1,0:T(8,128)S(1)}, f32[2,32,128]{2,1,0:T(8,128)S(1)}, u32[]{:S(2)}, u32[]{:S(2)}) %collective-permute-start.2) | collective-permute-done | bytes 32800 | tf_op jit(solution)/shard_map/ppermute | solution.py:299
  66.0 3.9 %all-to-all-done.3.raw = f32[32,1,3200]{2,1,0:T(1,128)S(1)} async-done(((f32[32,1,3200]{2,1,0:T(1,128)}), f32[32,1,3200]{2,1,0:T(1,128)S(1)}, u32[]{:S(2)}, u32[]{:S(2)}) %all-to-all-start.3) | async-done | bytes 409632 | tf_op jit(solution)/shard_map/all_to_all | solution.py:324
  69.8 0.0 copy-start
  69.8 5.2 %collective-permute-start.3 = (f32[32,1,3200]{2,1,0:T(1,128)S(1)}, f32[32,1,3200]{2,1,0:T(1,128)S(1)}, u32[]{:S(2)}, u32[]{:S(2)}) collective-permute-start(f32[32,1,3200]{2,1,0:T(1,128)S(1)} %all-to-all-done.3.raw), channel_id=1, source_target_pairs={{0,4},{4,0},{1,5},{5,1},{2,6},{6,2},{3,7},{7,3},{8,12},{12,8},{9,1... | collective-permute-start | bytes 1228808 | tf_op jit(solution)/shard_map/ppermute | solution.py:299
  75.0 1.9 %finish_first.1 = (bf16[2,128,3200]{2,1,0:T(8,128)(2,1)}, f32[2,1,128,3200]{3,2,1,0:T(8,128)}, f32[2,32,3200]{2,1,0:T(8,128)}) custom-call(s32[1]{0:T(128)} %bitcast.core_ref.which_ref, f32[32,1,3200]{2,1,0:T(1,128)S(1)} %all-to-all-done.3.raw, f32[2,32,128]{2,1,0:T(8,128)S(1)} %factor.1.factors, f32[128,3200]{1,0:T(8,128)S(1)} %get-tuple-element.31.c_own.c), custom_call_target="tpu_custom_call" | custom-call | flops 50000000 | bytes 6000000 | tf_op jit(solution)/shard_map/finish_first/pallas_call | solution.py:276
  76.9 0.0 collective-permute-done.3.raw
  76.9 0.0 copy-done
  77.0 1.9 %finish_second.1 = (bf16[2,128,3200]{2,1,0:T(8,128)(2,1)}, f32[2,1,128,3200]{3,2,1,0:T(8,128)}, f32[2,32,3200]{2,1,0:T(8,128)}) custom-call(s32[1]{0:T(128)S(6)} %sub.3.which_ref, f32[32,1,3200]{2,1,0:T(1,128)S(1)} %collective-permute-done.3.raw, ...), custom_call_target="tpu_custom_call", output_to_operand_aliasing={{0}: (4, {}), {1}: (5, {}), {2}: (6, {})} | custom-call | flops 50000000 | bytes 6000000 | tf_op jit(solution)/shard_map/finish_second/pallas_call | solution.py:276
  (4 shorter events, 0.1 us)
Async XLA Ops:
  3.5 4.5 %collective-permute-start = (f32[32,128]{1,0:T(8,128)S(1)}, f32[32,128]{1,0:T(8,128)S(1)}, u32[]{:S(2)}, u32[]{:S(2)}) collective-permute-start(f32[32,128]{1,0:T(8,128)S(1)} %get-tuple-element.28), channel_id=1, source_target_pairs={{0,4},{4,0},{1,5},{5,1},{2,6},{6,2},{3,7},{7,3},{8,12},{12,8},{9,1... | collective-permute-start | bytes 49160 | tf_op jit(solution)/shard_map/ppermute | solution.py:299
  8.0 28.5 %collective-permute-start.1 = (f32[128,3200]{1,0:T(8,128)}, f32[128,3200]{1,0:T(8,128)S(1)}, u32[]{:S(2)}, u32[]{:S(2)}) collective-permute-start(f32[128,3200]{1,0:T(8,128)} %get-tuple-element.32.c), channel_id=1, source_target_pairs={{0,4},{4,0},{1,5},{5,1},{2,6},{6,2},{3,7},{7,3},{8,12},{12,8},{9,1... | collective-permute-start | bytes 4915208 | tf_op jit(solution)/shard_map/ppermute | solution.py:299
  52.9 16.9 %all-to-all-start.3 = ((f32[32,1,3200]{2,1,0:T(1,128)}), f32[32,1,3200]{2,1,0:T(1,128)S(1)}, u32[]{:S(2)}, u32[]{:S(2)}) async-start(f32[32,1,3200]{2,1,0:T(1,128)} %spread.1), calls=%async_computation.3 | async-start | bytes 819200 | tf_op jit(solution)/shard_map/all_to_all | solution.py:324
  61.4 4.6 %collective-permute-start.2 = (f32[2,32,128]{2,1,0:T(8,128)S(1)}, f32[2,32,128]{2,1,0:T(8,128)S(1)}, u32[]{:S(2)}, u32[]{:S(2)}) collective-permute-start(f32[2,32,128]{2,1,0:T(8,128)S(1)} %factor.1.factors), channel_id=1, source_target_pairs={{0,4},{4,0},{1,5},{5,1},{2,6},{6,2},{3,7},{7,3},{8,12},{12,8},{9,1... | collective-permute-start | bytes 98312 | tf_op jit(solution)/shard_map/ppermute | solution.py:299
  69.8 7.1 %copy-start = (f32[128,3200]{1,0:T(8,128)S(1)}, f32[128,3200]{1,0:T(8,128)}, u32[]{:S(2)}) copy-start(f32[128,3200]{1,0:T(8,128)} %get-tuple-element.32.c) | copy-start | bytes 4915204
  69.8 7.1 %collective-permute-start.3 = (f32[32,1,3200]{2,1,0:T(1,128)S(1)}, f32[32,1,3200]{2,1,0:T(1,128)S(1)}, u32[]{:S(2)}, u32[]{:S(2)}) collective-permute-start(f32[32,1,3200]{2,1,0:T(1,128)S(1)} %all-to-all-done.3.raw), channel_id=1, source_target_pairs={{0,4},{4,0},{1,5},{5,1},{2,6},{6,2},{3,7},{7,3},{8,12},{12,8},{9,1... | collective-permute-start | bytes 1228808 | tf_op jit(solution)/shard_map/ppermute | solution.py:299

commit v8 on v7

--- a/solution.py
+++ b/solution.py
@@ -15,7 +15,7 @@
 PIECES = ((0, 1280), (1280, 1920))
 IN_PIECES = ((0, 1024), (1024, 1024), (2048, 768), (2816, 384))
 GROUPS = 4
-OUT_PIECES = ((0, 640), (640, 1280), (1920, 1280))
+OUT_PIECES = ((0, 896), (896, 896), (1792, 896), (2688, 512))
 VMEM_BYTES = 24 * 1024 * 1024
 
 

time: 79.2 us -> 79.3 us (level)
  no operation moved by 1% of the time
where the time goes in v8:
time: 79.3 us; the launch traced here: 78.9 us
  blocking collectives  43.2 us (54%)
  starting transfers between devices  17.6 us (22%)
  Pallas kernels  12.6 us (16%)
  waiting for transfers between devices  4.73 us (6%)
    all_to_all x2, blocking collectives, copies(): lax.all_to_all(jnp.broadcast_to(value[None], (count,) + value.shape), axe...  28.3 us
    all_to_all x1, blocking collectives, shards(): mine = spread(lax.all_to_all(raw, ('z', 'x'), 0, 0, tiled=True))  14.9 us
    ppermute x4, starting transfers between devices, swap(): return lax.ppermute(value, 'core', [(0, 1), (1, 0)])  12.4 us
    all_to_all x1, starting transfers between devices, shards(): raw = lax.all_to_all(mine, ('z', 'x'), 0, 0, tiled=True)  5.27 us
    pallas_call x2, Pallas kernels, finish(): pl.pallas_call(finish_kernel, in_specs=[SCALAR] + in_vmem(3) + anywhere(l...  3.88 us
    all_to_all x1, waiting for transfers between devices, shards(): raw = lax.all_to_all(mine, ('z', 'x'), 0, 0, tiled=True)  3.87 us
    pallas_call x1, Pallas kernels, factor(): pl.pallas_call(factor_kernel, in_specs=in_vmem(1), out_specs=in_vmem(1)[0...  3.15 us
    pallas_call x1, Pallas kernels, correct_other(): pl.pallas_call(other_kernel, in_specs=[SCALAR] + in_hbm(3), out_specs=in_...  2.86 us
  transfers between devices with their start and end apart: 5, of which 2 were waited for; matrix products, arithmetic and copies ran while one was open for 0% of the time, Pallas kernels for 8%

profile of v8, /device:TPU:1, one launch (start us, length us, event | category | flops | bytes accessed | tf_op | source)
XLA Modules:
  0.0 78.9 jit_solution(8852468221698562195)
XLA Ops:
  0.6 2.9 %correct_other.1 = (f32[128,3200]{1,0:T(8,128)S(1)}, f32[32,128]{1,0:T(8,128)S(1)}, bf16[128,3200]{1,0:T(8,128)(2,1)S(1)}, f32[128,3200]{1,0:T(8,128)S(1)}, f32[32,3200]{1,0:T(8,128)S(1)}) custom-call(s32[1]{0:T(128)} %bitcast.core_ref.which_ref, bf16[2,1,128,3200]{3,2,1,0:T(8,128)(2,1)} %grads.1, f32[2,1,128,3200]{3,2,1,0:T(8,128)} %errors.1, ...), custom_call_target="tpu_custom_call" | custom-call | flops 150000000 | bytes 9000000 | tf_op jit(solution)/shard_map/correct_other/pallas_call | solution.py:115
  3.5 3.3 %collective-permute-start = (f32[32,128]{1,0:T(8,128)S(1)}, f32[32,128]{1,0:T(8,128)S(1)}, u32[]{:S(2)}, u32[]{:S(2)}) collective-permute-start(f32[32,128]{1,0:T(8,128)S(1)} %get-tuple-element.28), channel_id=1, source_target_pairs={{0,4},{4,0},{1,5},{5,1},{2,6},{6,2},{3,7},{7,3},{8,12},{12,8},{9,1... | collective-permute-start | bytes 49160 | tf_op jit(solution)/shard_map/ppermute | solution.py:299
  6.8 1.2 %correct_own.1 = (f32[128,3200]{1,0:T(8,128)S(1)}, f32[32,128]{1,0:T(8,128)S(1)}, f32[128,3200]{1,0:T(8,128)}) custom-call(bf16[128,3200]{1,0:T(8,128)(2,1)S(1)} %get-tuple-element.23.g, f32[128,3200]{1,0:T(8,128)S(1)} %get-tuple-element.24.e, f32[32,3200]{1,0:T(8,128)S(1)} %get-tuple-element.25.q, f32[128,3200]{1,0:T(8,128)S(1)} %get-tuple-element.26.c_oth), custom_call_target="tpu_custom_call" | custom-call | flops 150000000 | bytes 4000000 | tf_op jit(solution)/shard_map/correct_own/pallas_call | solution.py:139
  8.0 0.0 collective-permute-done
  8.0 0.1 collective-permute-start.1
  8.2 12.3 %all_to_all.20 = f32[16,32,128]{2,1,0:T(8,128)S(1)} all-to-all(f32[16,32,128]{2,1,0:T(8,128)S(1)} %broadcast_in_dim.7), channel_id=1, replica_groups=mesh['z'=8,'x'=4,'core'=2,'tensor'=4] {'x','tensor'}, dimensions={0} | all-to-all | bytes 524288 | tf_op jit(solution)/shard_map/all_to_all | solution.py:306
  20.5 16.0 %all_to_all.21.parts = f32[8,32,128]{2,1,0:T(8,128)S(1)} all-to-all(f32[8,32,128]{2,1,0:T(8,128)S(1)} %broadcast_in_dim.8), channel_id=1, replica_groups=mesh['z'=8,'x'=4,'core'=2,'tensor'=4] {'z'}, dimensions={0} | all-to-all | bytes 262144 | tf_op jit(solution)/shard_map/all_to_all | solution.py:306
  36.5 0.0 collective-permute-done.1.c_got
  36.5 0.5 right_terms.1
  37.0 14.9 %all_to_all.22.parts = f32[32,1,3200]{2,1,0:T(1,128)S(1)} all-to-all(f32[32,1,3200]{2,1,0:T(1,128)S(1)} %get-tuple-element.33), channel_id=1, replica_groups=mesh['z'=8,'x'=4,'core'=2,'tensor'=4] {'z','x'}, dimensions={0} | all-to-all | bytes 819200 | tf_op jit(solution)/shard_map/all_to_all | solution.py:320
  51.9 1.0 %spread.1 = f32[32,1,3200]{2,1,0:T(1,128)} custom-call(f32[32,1,3200]{2,1,0:T(1,128)S(1)} %all_to_all.22.parts), custom_call_target="tpu_custom_call" | custom-call | flops 100000 | bytes 1000000 | tf_op jit(solution)/shard_map/spread/pallas_call | solution.py:194
  52.9 5.3 %all-to-all-start.3 = ((f32[32,1,3200]{2,1,0:T(1,128)}), f32[32,1,3200]{2,1,0:T(1,128)S(1)}, u32[]{:S(2)}, u32[]{:S(2)}) async-start(f32[32,1,3200]{2,1,0:T(1,128)} %spread.1), calls=%async_computation.3 | async-start | bytes 819200 | tf_op jit(solution)/shard_map/all_to_all | solution.py:324
  58.2 3.1 %factor.1.factors = f32[2,32,128]{2,1,0:T(8,128)S(1)} custom-call(f32[32,128]{1,0:T(8,128)S(1)} %get-tuple-element.36.left_ref), custom_call_target="tpu_custom_call" | custom-call | flops 10000000 | bytes 10000000 | tf_op jit(solution)/shard_map/factor/pallas_call | solution.py:239
  61.4 3.7 %collective-permute-start.2 = (f32[2,32,128]{2,1,0:T(8,128)S(1)}, f32[2,32,128]{2,1,0:T(8,128)S(1)}, u32[]{:S(2)}, u32[]{:S(2)}) collective-permute-start(f32[2,32,128]{2,1,0:T(8,128)S(1)} %factor.1.factors), channel_id=1, source_target_pairs={{0,4},{4,0},{1,5},{5,1},{2,6},{6,2},{3,7},{7,3},{8,12},{12,8},{9,1... | collective-permute-start | bytes 98312 | tf_op jit(solution)/shard_map/ppermute | solution.py:299
  65.1 0.9 %collective-permute-done.2.factors = f32[2,32,128]{2,1,0:T(8,128)S(1)} collective-permute-done((f32[2,32,128]{2,1,0:T(8,128)S(1)}, f32[2,32,128]{2,1,0:T(8,128)S(1)}, u32[]{:S(2)}, u32[]{:S(2)}) %collective-permute-start.2) | collective-permute-done | bytes 32800 | tf_op jit(solution)/shard_map/ppermute | solution.py:299
  66.0 3.9 %all-to-all-done.3.raw = f32[32,1,3200]{2,1,0:T(1,128)S(1)} async-done(((f32[32,1,3200]{2,1,0:T(1,128)}), f32[32,1,3200]{2,1,0:T(1,128)S(1)}, u32[]{:S(2)}, u32[]{:S(2)}) %all-to-all-start.3) | async-done | bytes 409632 | tf_op jit(solution)/shard_map/all_to_all | solution.py:324
  69.8 0.0 copy-start
  69.8 5.2 %collective-permute-start.3 = (f32[32,1,3200]{2,1,0:T(1,128)S(1)}, f32[32,1,3200]{2,1,0:T(1,128)S(1)}, u32[]{:S(2)}, u32[]{:S(2)}) collective-permute-start(f32[32,1,3200]{2,1,0:T(1,128)S(1)} %all-to-all-done.3.raw), channel_id=1, source_target_pairs={{0,4},{4,0},{1,5},{5,1},{2,6},{6,2},{3,7},{7,3},{8,12},{12,8},{9,1... | collective-permute-start | bytes 1228808 | tf_op jit(solution)/shard_map/ppermute | solution.py:299
  75.0 1.9 %finish_first.1 = (bf16[2,128,3200]{2,1,0:T(8,128)(2,1)}, f32[2,1,128,3200]{3,2,1,0:T(8,128)}, f32[2,32,3200]{2,1,0:T(8,128)}) custom-call(s32[1]{0:T(128)} %bitcast.core_ref.which_ref, f32[32,1,3200]{2,1,0:T(1,128)S(1)} %all-to-all-done.3.raw, f32[2,32,128]{2,1,0:T(8,128)S(1)} %factor.1.factors, f32[128,3200]{1,0:T(8,128)S(1)} %get-tuple-element.31.c_own.c), custom_call_target="tpu_custom_call" | custom-call | flops 50000000 | bytes 6000000 | tf_op jit(solution)/shard_map/finish_first/pallas_call | solution.py:276
  77.0 0.0 collective-permute-done.3.raw
  77.0 0.0 copy-done
  77.0 1.9 %finish_second.1 = (bf16[2,128,3200]{2,1,0:T(8,128)(2,1)}, f32[2,1,128,3200]{3,2,1,0:T(8,128)}, f32[2,32,3200]{2,1,0:T(8,128)}) custom-call(s32[1]{0:T(128)S(6)} %sub.3.which_ref, f32[32,1,3200]{2,1,0:T(1,128)S(1)} %collective-permute-done.3.raw, ...), custom_call_target="tpu_custom_call", output_to_operand_aliasing={{0}: (4, {}), {1}: (5, {}), {2}: (6, {})} | custom-call | flops 50000000 | bytes 6000000 | tf_op jit(solution)/shard_map/finish_second/pallas_call | solution.py:276
  (4 shorter events, 0.1 us)
Async XLA Ops:
  3.5 4.5 %collective-permute-start = (f32[32,128]{1,0:T(8,128)S(1)}, f32[32,128]{1,0:T(8,128)S(1)}, u32[]{:S(2)}, u32[]{:S(2)}) collective-permute-start(f32[32,128]{1,0:T(8,128)S(1)} %get-tuple-element.28), channel_id=1, source_target_pairs={{0,4},{4,0},{1,5},{5,1},{2,6},{6,2},{3,7},{7,3},{8,12},{12,8},{9,1... | collective-permute-start | bytes 49160 | tf_op jit(solution)/shard_map/ppermute | solution.py:299
  8.0 28.5 %collective-permute-start.1 = (f32[128,3200]{1,0:T(8,128)}, f32[128,3200]{1,0:T(8,128)S(1)}, u32[]{:S(2)}, u32[]{:S(2)}) collective-permute-start(f32[128,3200]{1,0:T(8,128)} %get-tuple-element.32.c), channel_id=1, source_target_pairs={{0,4},{4,0},{1,5},{5,1},{2,6},{6,2},{3,7},{7,3},{8,12},{12,8},{9,1... | collective-permute-start | bytes 4915208 | tf_op jit(solution)/shard_map/ppermute | solution.py:299
  52.9 16.9 %all-to-all-start.3 = ((f32[32,1,3200]{2,1,0:T(1,128)}), f32[32,1,3200]{2,1,0:T(1,128)S(1)}, u32[]{:S(2)}, u32[]{:S(2)}) async-start(f32[32,1,3200]{2,1,0:T(1,128)} %spread.1), calls=%async_computation.3 | async-start | bytes 819200 | tf_op jit(solution)/shard_map/all_to_all | solution.py:324
  61.4 4.6 %collective-permute-start.2 = (f32[2,32,128]{2,1,0:T(8,128)S(1)}, f32[2,32,128]{2,1,0:T(8,128)S(1)}, u32[]{:S(2)}, u32[]{:S(2)}) collective-permute-start(f32[2,32,128]{2,1,0:T(8,128)S(1)} %factor.1.factors), channel_id=1, source_target_pairs={{0,4},{4,0},{1,5},{5,1},{2,6},{6,2},{3,7},{7,3},{8,12},{12,8},{9,1... | collective-permute-start | bytes 98312 | tf_op jit(solution)/shard_map/ppermute | solution.py:299
  69.8 7.2 %copy-start = (f32[128,3200]{1,0:T(8,128)S(1)}, f32[128,3200]{1,0:T(8,128)}, u32[]{:S(2)}) copy-start(f32[128,3200]{1,0:T(8,128)} %get-tuple-element.32.c) | copy-start | bytes 4915204
  69.8 7.1 %collective-permute-start.3 = (f32[32,1,3200]{2,1,0:T(1,128)S(1)}, f32[32,1,3200]{2,1,0:T(1,128)S(1)}, u32[]{:S(2)}, u32[]{:S(2)}) collective-permute-start(f32[32,1,3200]{2,1,0:T(1,128)S(1)} %all-to-all-done.3.raw), channel_id=1, source_target_pairs={{0,4},{4,0},{1,5},{5,1},{2,6},{6,2},{3,7},{7,3},{8,12},{12,8},{9,1... | collective-permute-start | bytes 1228808 | tf_op jit(solution)/shard_map/ppermute | solution.py:299
